TPU v7x, 128 devices: a whole 4x4x4 slice. The times are simulated.
128 devices in a mesh: band: 16 (over z, y_hi, core), ga: 8 (over y_lo, x).
Axes of the slice: x: 4, y: 4 (y_hi: 2, y_lo: 2; y = y_hi * 2 + y_lo), z: 4, core: 2. Of those that a mesh axis runs over, the one named last changes fastest.
Arguments:
- trial_bands: float32 [16, 2, 160, 5120], P('band', None, None, 'ga'), may hold values from -6 to 6
- basis_bands: float32 [16, 2, 160, 5120], P('band', None, None, 'ga'), may hold values from -6 to 6
- column_sites: int32 [5120], replicated, may hold values from 0 to 25599, as said below
- potential: float32 [160, 160, 160], P('ga'), may hold values from -1.5 to 0.5
- box_cells: int32 [1536, 128], P('ga'), may hold values from 0 to 511999, as said below
- box_atom: int32 [1536], P('ga'), may hold values from 0 to 1023, as said below
- box_beta: float32 [1536, 128], P('ga'), may hold values from -0.5 to 0.5
- strength: float32 [1024], replicated, may hold values from 2 to 8
Outputs:
- applied_bands: float32 [16, 2, 160, 5120], P('band', None, None, 'ga')
- gram_block: float32 [2, 16, 16], P(None, None, 'band')
Inputs may be any that keep to these rules, and one draw needn't show every extreme that they name: `column_sites`: distinct positions; the first and the last position of a plane are among them. `box_cells`: each row is a box of 2 planes by 8 by 8 cells inside its device's own 20 planes, the in-plane indices wrapping around the grid; a cell is plane * 160 * 160 + x * 160 + y within that block of planes; entry j of a row is the cell at planes, x and y offsets (j // 64, (j // 8) % 8, j % 8) from the row's entry 0, x and y taken modulo 160. `box_atom`: an atom may own blocks on several devices or on none.
All inputs are finite; a program needn't handle non-finite values.
Results may differ from a plain program's by a relative error of at most 0.00011.
Values sent between devices are 32-bit elements; how exact they have to be, the bound alone decides.
No kernel may reach another device: no remote copies, remote signals or barrier semaphores. Data moves between devices by JAX's collectives and lax.ppermute only.
A program may use at most 192 MiB of HBM per device.

v0:
```python
import math

import jax
import jax.numpy as jnp
from jax import lax
from jax.sharding import PartitionSpec as P

highest = lax.Precision.HIGHEST


def tables(length):
    index = jnp.arange(length, dtype=jnp.int32)
    phase = index[:, None] * index[None, :] % length
    angle = phase.astype(jnp.float32) * (2.0 * math.pi / length)
    return (jnp.cos(angle), jnp.sin(angle))


def frequency(index, length):
    return jnp.where(index < length // 2, index, index - length).astype(jnp.float32)


def along_depth(real_part, imag_part, cosine, sine_table, orient):
    real_cos = jnp.einsum("pzc,zq->pqc", real_part, cosine, precision=highest)
    imag_sin = jnp.einsum("pzc,zq->pqc", imag_part, sine_table, precision=highest)
    imag_cos = jnp.einsum("pzc,zq->pqc", imag_part, cosine, precision=highest)
    real_sin = jnp.einsum("pzc,zq->pqc", real_part, sine_table, precision=highest)
    return (real_cos - orient * imag_sin, imag_cos + orient * real_sin)


def inner_table(cosine, sine_table, orient):
    upper = jnp.concatenate([cosine, orient * sine_table], axis=1)
    lower = jnp.concatenate([-orient * sine_table, cosine], axis=1)
    return jnp.concatenate([upper, lower], axis=0)


def along_inner(slab, table):
    return jnp.matmul(slab, table, precision=highest)


def along_outer(slab, stacked, orient, length):
    mixed = jnp.einsum("qx,pxk->pqk", stacked, slab, precision=highest)
    first = mixed[:, :length]
    second = mixed[:, length:]
    real_part = first[:, :, :length] - orient * second[:, :, length:]
    imag_part = first[:, :, length:] + orient * second[:, :, :length]
    return jnp.concatenate([real_part, imag_part], axis=2)


def gram_terms(left, right):
    real_sum = jnp.einsum("izc,jzc->ij", left[:, 0], right[:, 0], precision=highest) + jnp.einsum(
        "izc,jzc->ij", left[:, 1], right[:, 1], precision=highest
    )
    imag_sum = jnp.einsum("izc,jzc->ij", left[:, 0], right[:, 1], precision=highest) - jnp.einsum(
        "izc,jzc->ij", left[:, 1], right[:, 0], precision=highest
    )
    return jnp.stack([real_sum, imag_sum])


def on_device(
    trial_bands, basis_bands, column_sites, potential, box_cells, box_atom, box_beta, strength
):
    length = trial_bands.shape[2]
    local_columns = trial_bands.shape[3]
    planes = potential.shape[0]
    atom_count = strength.shape[0]
    site_count = column_sites.shape[0]
    block_rows = box_cells.shape[0]
    cosine, sine_table = tables(length)
    grid_total = float(length**3)
    forward_inner = inner_table(cosine, sine_table, 1.0)
    backward_inner = inner_table(cosine, sine_table, -1.0)
    stacked = jnp.concatenate([cosine, sine_table], axis=0)
    wide = 2 * length
    site_row = column_sites // length
    site_col = column_sites % length
    placed_sites = jnp.concatenate(
        [site_row * wide + site_col, site_row * wide + length + site_col]
    )
    corner = box_cells[:, 0]
    plane_start = corner // (length * length)
    row_start = corner // length % length
    col_start = corner % length
    line_offsets = jnp.arange(16, dtype=jnp.int32)
    line_index = (plane_start[:, None] + line_offsets[None, :] // 8) * length + (
        row_start[:, None] + line_offsets[None, :] % 8
    ) % length
    window_cols = (col_start[:, None] + jnp.arange(8, dtype=jnp.int32)[None, :]) % length
    window = (jnp.arange(length, dtype=jnp.int32)[None, :, None] == window_cols[:, None, :]).astype(
        jnp.float32
    )
    doubled_potential = jnp.concatenate([potential, potential], axis=2).reshape(
        planes * length, wide
    )

    def depth_transform(values, orient):
        real_part, imag_part = along_depth(values[:, 0], values[:, 1], cosine, sine_table, orient)
        return jnp.stack([real_part, imag_part], axis=1)

    columns = depth_transform(trial_bands, 1.0)
    items = lax.all_to_all(columns, "ga", split_axis=2, concat_axis=3, tiled=True)
    count_items = items.shape[0]
    values = jnp.concatenate([items[:, 0], items[:, 1]], axis=2)
    placed = (
        jnp.zeros((count_items, planes, length * wide), jnp.float32)
        .at[:, :, placed_sites]
        .set(values)
    )
    slab = along_inner(placed.reshape(count_items * planes, length, wide), forward_inner)
    slab = along_outer(slab, stacked, 1.0, length)
    field = slab.reshape(count_items, planes * length, wide)
    lines = jnp.take(field, line_index, axis=1).reshape(count_items, block_rows, 16, 2, length)
    box_values = jnp.einsum("islpy,syj->ipslj", lines, window, precision=highest).reshape(
        count_items, 2, block_rows, 128
    )
    partial_value = jnp.sum(box_values * box_beta, axis=3)
    gathered = partial_value.reshape(count_items * 2, -1)
    projected = jax.ops.segment_sum(gathered.T, box_atom, num_segments=atom_count).T
    projected = lax.psum(projected, "ga")
    weights = (strength * projected)[:, box_atom].reshape(count_items, 2, -1)
    added = (weights[:, :, :, None] * box_beta).reshape(count_items, 2, block_rows, 16, 8)
    spread = jnp.einsum("ipslj,syj->islpy", added, window, precision=highest).reshape(
        count_items, block_rows, 16, wide
    )
    out_field = (field * doubled_potential).at[:, line_index].add(spread)
    slab = along_inner(out_field.reshape(count_items * planes, length, wide), backward_inner)
    slab = along_outer(slab, stacked, -1.0, length)
    picked = slab.reshape(count_items, planes, length * wide)[:, :, placed_sites]
    picked = picked.reshape(count_items, planes, 2, site_count).transpose(0, 2, 1, 3)
    returned = lax.all_to_all(picked, "ga", split_axis=3, concat_axis=2, tiled=True)
    spectrum = depth_transform(returned, -1.0) / grid_total
    own_sites = lax.dynamic_slice_in_dim(
        column_sites, lax.axis_index("ga") * local_columns, local_columns
    )
    axis_freq = frequency(jnp.arange(length, dtype=jnp.int32), length)
    freq_x = frequency(own_sites // length, length)
    freq_y = frequency(own_sites % length, length)
    kinetic = (
        2.0
        * (axis_freq[:, None] ** 2 + freq_x[None, :] ** 2 + freq_y[None, :] ** 2)
        / float(length * length)
    )
    applied = spectrum + kinetic * trial_bands
    norm = 1.0 / math.sqrt(length * local_columns * lax.axis_size("ga"))
    partial_gram = gram_terms(lax.all_gather(basis_bands, "band", axis=0, tiled=True), applied)
    gram_block = lax.psum(partial_gram, "ga") * norm
    return (applied, gram_block)


def solution(mesh):
    placed = (
        P("band", None, None, "ga"),
        P("band", None, None, "ga"),
        P(),
        P("ga", None, None),
        P("ga", None),
        P("ga"),
        P("ga", None),
        P(),
    )
    return jax.shard_map(
        on_device,
        mesh=mesh,
        in_specs=placed,
        out_specs=(P("band", None, None, "ga"), P(None, None, "band")),
        check_vma=False,
    )
```

profile of v0, /device:TPU:0, one launch (start us, length us, event | category | flops | bytes accessed | tf_op | source)
XLA Modules:
  0.0 481.4 jit_solution(8724639003103221340)
XLA Ops:
  27.7 10.5 %all-to-all-done = f32[1,2,160,640]{3,1,0,2:T(2,128)S(1)} async-done(((f32[1,2,160,640]{3,1,0,2:T(2,128)}), f32[1,2,160,640]{3,1,0,2:T(2,128)S(1)}, u32[]{:S(2)}, u32[]{:S(2)}) %all-to-all-start) | async-done | bytes 819232 | tf_op jit(solution)/shard_map/all_to_all | solution.py:100
  43.4 37.0 %scatter_custom_fusion = f32[20,51200]{0,1:T(8,128)} fusion(s32[10240]{0:T(1024)S(1)} %bitcast.160, f32[]{:T(128)} %constant.140.clone.1, f32[1,20,10240]{1,2,0:T(8,128)} %copy.101), kind=kCustom, calls=%fused_computation.6 | custom fusion | bytes 4915204 | tf_op jit(solution)/shard_map/scatter | solution.py:106
  80.4 16.6 %copy.73 = f32[20,160,320]{2,1,0:T(8,128)} copy(f32[20,160,320]{0,2,1:T(8,128)} %bitcast.148) | data formatting | bytes 8192000 | tf_op jit(solution)/shard_map/reshape | solution.py:108
  97.0 11.8 %fusion.59 = f32[20,160,320]{2,1,0:T(8,128)S(1)} fusion(f32[20,160,320]{2,1,0:T(8,128)} %copy.73, f32[160,160]{1,0:T(8,128)S(1)} %get-tuple-element.24, f32[160,160]{1,0:T(8,128)S(1)} %broadcast_multiply_fusion.1, f32[160,160]{1,0:T(8,128)S(1)} %get-tuple-element.23), kind=kOutput, calls=%fused_computation.72 | convolution fusion | flops 3932467200 | bytes 8499200 | tf_op jit(solution)/shard_map/dot_general | solution.py:37
  108.8 9.0 %convolution_bitcast_fusion.1 = f32[20,320,320]{2,1,0:T(8,128)S(1)} fusion(f32[20,160,320]{2,1,0:T(8,128)S(1)} %fusion.59, f32[160,160]{1,0:T(8,128)S(1)} %get-tuple-element.23, f32[160,160]{1,0:T(8,128)S(1)} %get-tuple-element.24), kind=kOutput, calls=%fused_computation.27 | convolution fusion | flops 3932211200 | bytes 12492800 | tf_op jit(solution)/shard_map/qx,pxk->pqk/dot_general | solution.py:41
  127.5 15.5 %gather_fusion = f32[3072,320]{1,0:T(8,128)} fusion(f32[3200,320]{1,0:T(8,128)} %bitcast.147, s32[3072]{0:T(1024)S(1)} %broadcast_clamp_fusion.1), kind=kCustom, calls=%fused_computation | custom fusion | bytes 7876608 | tf_op jit(solution)/shard_map/jit(_take)/gather | solution.py:111
  142.9 9.2 %gather.13 = f32[192,16,2,160]{3,2,1,0:T(2,128)} reshape(f32[3072,320]{1,0:T(8,128)} %gather_fusion) | data formatting | bytes 7864320 | tf_op jit(solution)/shard_map/jit(_take)/gather | solution.py:111
  158.3 11.4 %fusion.15 = f32[2,192]{0,1:T(8,128)S(1)} fusion(f32[192,16,2,160]{3,2,1,0:T(2,128)S(1)} %broadcast_select_fusion, f32[192,16,8]{1,2,0:T(8,128)S(1)} %copy.78, s32[192,8]{1,0:T(8,128)S(1)} %copy-done.7), kind=kOutput, calls=%fused_computation.36 | convolution fusion | flops 94715520 | bytes 4038144 | tf_op jit(solution)/shard_map/islpy,syj->ipslj/dot_general | solution.py:112
  171.0 38.1 %psum.14 = f32[2,1024]{0,1:T(8,128)S(1)} all-reduce(f32[2,1024]{0,1:T(8,128)S(1)} %bitcast.157), channel_id=1, replica_groups=mesh['band'=16,'ga'=8] {'ga'}, use_global_device_ids=true, to_apply=%region_3.4 | all-reduce | flops 2048 | bytes 16384 | tf_op jit(solution)/shard_map/psum | solution.py:118
  233.2 24.2 %scatter_fusion = f32[3200,320]{1,0:T(8,128)} fusion(f32[3200,320]{1,0:T(8,128)} %bitcast.145, s32[3072]{0:T(1024)S(1)} %reshape.618, f32[3072,320]{1,0:T(8,128)} %reshape.620), kind=kCustom, calls=%fused_computation.5 | custom fusion | flops 983040 | bytes 11808768 | tf_op jit(solution)/shard_map/scatter-add | solution.py:124
  257.3 12.0 %fusion.63 = f32[20,160,320]{2,1,0:T(8,128)S(1)} fusion(f32[20,160,320]{2,1,0:T(8,128)} %bitcast.146, f32[160,160]{1,0:T(8,128)S(1)} %get-tuple-element.24, f32[160,160]{1,0:T(8,128)S(1)} %get-tuple-element.23, f32[160,160]{1,0:T(8,128)S(1)} %copy-done.6), kind=kOutput, calls=%fused_computation.75 | convolution fusion | flops 3932467200 | bytes 8499200 | tf_op jit(solution)/shard_map/dot_general | solution.py:37
  269.3 9.0 %convolution_bitcast_fusion = f32[20,320,320]{2,1,0:T(8,128)S(1)} fusion(f32[20,160,320]{2,1,0:T(8,128)S(1)} %fusion.63, f32[160,160]{1,0:T(8,128)S(1)} %get-tuple-element.23, f32[160,160]{1,0:T(8,128)S(1)} %get-tuple-element.24), kind=kOutput, calls=%fused_computation.26 | convolution fusion | flops 3932211200 | bytes 12492800 | tf_op jit(solution)/shard_map/qx,pxk->pqk/dot_general | solution.py:41
  283.3 14.4 %copy.95 = f32[20,160,320]{0,2,1:T(8,128)} copy(f32[20,160,320]{2,1,0:T(8,128)} %pad_maximum_fusion.1) | data formatting | bytes 8192000 | tf_op jit(solution)/shard_map/reshape | solution.py:127
  297.7 42.6 %gather_fusion.2 = f32[10240,20]{1,0:T(8,128)} fusion(f32[20,51200]{0,1:T(8,128)} %bitcast.149, s32[10240]{0:T(1024)S(1)} %broadcast_clamp_fusion), kind=kCustom, calls=%fused_computation.2 | custom fusion | bytes 1679360 | tf_op jit(solution)/shard_map/gather | solution.py:127
  340.4 10.6 %copy.158 = f32[1,20,2,5120]{1,2,0,3:T(2,128)} copy(f32[1,20,2,5120]{1,3,2,0:T(8,128)} %bitcast.152) | data formatting | bytes 1638400 | tf_op jit(solution)/shard_map/reshape | solution.py:128
  351.0 10.6 %reshape.657 = f32[8,1,25600]{2,1,0:T(1,128)} reshape(f32[5120,1,2,20]{3,2,1,0:T(2,128)} %bitcast.150) | data formatting | bytes 1638400
  365.4 10.0 %all-to-all-done.1 = f32[8,1,25600]{2,1,0:T(1,128)S(1)} async-done(((f32[8,1,25600]{2,1,0:T(1,128)}), f32[8,1,25600]{2,1,0:T(1,128)S(1)}, u32[]{:S(2)}, u32[]{:S(2)}) %all-to-all-start.1) | async-done | bytes 819232 | tf_op jit(solution)/shard_map/all_to_all | solution.py:129
  378.6 10.9 %reshape.658 = f32[5120,1,2,20]{3,2,1,0:T(2,128)} reshape(f32[8,25600]{1,0:T(8,128)S(1)} %reduce.8) | data formatting | bytes 1638400
  400.9 10.5 %slice_bitcast_fusion = (f32[16,160,640]{2,1,0:T(8,128)}, f32[16,160,640]{2,1,0:T(8,128)}) fusion(f32[16,2,160,640]{3,2,1,0:T(8,128)} %all-gather.2.cloned.1.call-done), kind=kLoop, calls=%fused_computation.8 | loop fusion | bytes 26214400 | tf_op jit(solution)/shard_map/squeeze | solution.py:51
  411.4 12.1 %fusion.24 = f32[16]{0:T(128)S(1)} fusion(f32[16,160,640]{2,1,0:T(8,128)} %get-tuple-element.8, f32[160,640,1]{1,0,2:T(8,128)S(1)} %get-tuple-element.13), kind=kOutput, calls=%fused_computation.50 | convolution fusion | flops 19660800 | bytes 6963264 | tf_op jit(solution)/shard_map/izc,jzc->ij/dot_general | solution.py:50
  423.5 10.8 %fusion.27 = f32[16]{0:T(128)S(1)} fusion(f32[16,160,640]{2,1,0:T(8,128)S(1)} %copy-done.1, f32[160,640,1]{1,0,2:T(8,128)S(1)} %get-tuple-element.14), kind=kOutput, calls=%fused_computation.51 | convolution fusion | flops 19660800 | bytes 6963264 | tf_op jit(solution)/shard_map/izc,jzc->ij/dot_general | solution.py:53
  434.3 11.0 %fusion.45 = f32[1,16,1]{1,2,0:T(1,128)S(1)} fusion(f32[16]{0:T(128)S(1)} %fusion.24, f32[16,160,640]{2,1,0:T(8,128)S(1)} %copy-done, f32[160,640,1]{1,0,2:T(8,128)S(1)} %get-tuple-element.14), kind=kOutput, calls=%fused_computation.57 | convolution fusion | flops 19660816 | bytes 6963328 | tf_op jit(solution)/shard_map/izc,jzc->ij/dot_general | solution.py:50
  445.3 11.0 %fusion.39 = f32[1,16,1]{1,2,0:T(1,128)S(1)} fusion(f32[16]{0:T(128)S(1)} %fusion.27, f32[16,160,640]{2,1,0:T(8,128)S(1)} %copy-done, f32[160,640,1]{1,0,2:T(8,128)S(1)} %get-tuple-element.13), kind=kOutput, calls=%fused_computation.55 | convolution fusion | flops 19660816 | bytes 6963328 | tf_op jit(solution)/shard_map/izc,jzc->ij/dot_general | solution.py:53
  456.3 17.4 %psum.15 = f32[2,16,1]{1,2,0:T(1,128)S(1)} all-reduce(f32[2,16,1]{1,2,0:T(1,128)S(1)} %pad_maximum_fusion.10), channel_id=1, replica_groups=mesh['band'=16,'ga'=8] {'ga'}, use_global_device_ids=true, to_apply=%region_5.6 | all-reduce | flops 32 | bytes 256 | tf_op jit(solution)/shard_map/psum | solution.py:145
  (85 shorter events, 90.6 us)
Async XLA Ops:
  7.2 16.9 %copy-start.9 = (s32[192,128]{1,0:T(8,128)S(1)}, s32[192,128]{1,0:T(8,128)}, u32[]{:S(2)}) copy-start(s32[192,128]{1,0:T(8,128)} %param.12) | copy-start | bytes 294916
  7.2 393.7 %all-gather.2.cloned.1.call-start = ((), (), s32[]{:S(2)}) async-start(), calls=%async_computation.2 | async-start | bytes 13926400 | tf_op jit(solution)/shard_map/all_gather | solution.py:144
  7.9 18.1 %copy-start.12 = (s32[192]{0:T(256)S(1)}, s32[192]{0:T(256)}, u32[]{:S(2)}) copy-start(s32[192]{0:T(256)} %param.13) | copy-start | bytes 2308
  7.9 18.2 %copy-start.10 = (s32[5120]{0:T(1024)S(1)}, s32[5120]{0:T(1024)}, u32[]{:S(2)}) copy-start(s32[5120]{0:T(1024)} %param.10) | copy-start | bytes 61444
  7.9 18.5 %copy-start.8 = (f32[192,128]{1,0:T(8,128)S(1)}, f32[192,128]{1,0:T(8,128)}, u32[]{:S(2)}) copy-start(f32[192,128]{1,0:T(8,128)} %param.14) | copy-start | bytes 294916
  18.5 19.7 %all-to-all-start = ((f32[1,2,160,640]{3,1,0,2:T(2,128)}), f32[1,2,160,640]{3,1,0,2:T(2,128)S(1)}, u32[]{:S(2)}, u32[]{:S(2)}) async-start(f32[1,2,160,640]{3,1,0,2:T(2,128)} %copy.69), calls=%async_computation | async-start | bytes 1638400 | tf_op jit(solution)/shard_map/all_to_all | solution.py:100
  25.3 71.6 %copy-start.5 = (f32[160,160]{1,0:T(8,128)}, f32[160,160]{1,0:T(8,128)S(1)}, u32[]{:S(2)}) copy-start(f32[160,160]{1,0:T(8,128)S(1)} %broadcast_multiply_fusion.1) | copy-start | bytes 307204
  26.8 131.4 %copy-start.3 = (f32[192,16,8]{1,2,0:T(8,128)}, f32[192,16,8]{1,2,0:T(8,128)S(1)}, u32[]{:S(2)}) copy-start(f32[192,16,8]{1,2,0:T(8,128)S(1)} %copy.78) | copy-start | bytes 294916
  152.1 6.1 %copy-start.7 = (s32[192,8]{1,0:T(8,128)S(1)}, s32[192,8]{1,0:T(8,128)}, u32[]{:S(2)}) copy-start(s32[192,8]{1,0:T(8,128)} %add_select_fusion.1) | copy-start | bytes 18436
  158.2 50.8 %copy-start.11 = (f32[1024]{0:T(1024)S(1)}, f32[1024]{0:T(1024)}, u32[]{:S(2)}) copy-start(f32[1024]{0:T(1024)} %param.15) | copy-start | bytes 12292
  233.2 24.2 %copy-start.6 = (f32[160,160]{1,0:T(8,128)S(1)}, f32[160,160]{1,0:T(8,128)}, u32[]{:S(2)}) copy-start(f32[160,160]{1,0:T(8,128)} %copy-done.5) | copy-start | bytes 307204
  361.5 13.9 %all-to-all-start.1 = ((f32[8,1,25600]{2,1,0:T(1,128)}), f32[8,1,25600]{2,1,0:T(1,128)S(1)}, u32[]{:S(2)}, u32[]{:S(2)}) async-start(f32[8,1,25600]{2,1,0:T(1,128)} %reshape.657), calls=%async_computation.1 | async-start | bytes 1638400 | tf_op jit(solution)/shard_map/all_to_all | solution.py:129
  394.6 6.0 %copy-start.2 = (f32[1,2,160,640]{3,2,1,0:T(8,128)S(1)}, f32[1,2,160,640]{3,2,1,0:T(8,128)}, u32[]{:S(2)}) copy-start(f32[1,2,160,640]{3,2,1,0:T(8,128)} %param.8) | copy-start | bytes 2457604
  400.8 10.6 %copy-start.4 = (f32[1,2,160,640]{3,2,1,0:T(8,128)}, f32[1,2,160,640]{3,2,1,0:T(8,128)S(1)}, u32[]{:S(2)}) copy-start(f32[1,2,160,640]{3,2,1,0:T(8,128)S(1)} %fusion.52) | copy-start | bytes 2457604
  411.4 12.1 %copy-start.1 = (f32[16,160,640]{2,1,0:T(8,128)S(1)}, f32[16,160,640]{2,1,0:T(8,128)}, u32[]{:S(2)}) copy-start(f32[16,160,640]{2,1,0:T(8,128)} %get-tuple-element.8) | copy-start | bytes 19660804
  423.5 10.8 %copy-start = (f32[16,160,640]{2,1,0:T(8,128)S(1)}, f32[16,160,640]{2,1,0:T(8,128)}, u32[]{:S(2)}) copy-start(f32[16,160,640]{2,1,0:T(8,128)} %get-tuple-element.7) | copy-start | bytes 19660804
Sparse Core Ops, SparseCore 0:
  10.5 104.3 all-gather.1
where the time goes:
time: 488 us; the launch traced here: 481 us
  local copies, waits for them, and re-layouts  210 us (43%)
  matrix products  117 us (24%)
  blocking collectives  55.5 us (11%)
  other arithmetic  53.6 us (11%)
  waiting for transfers between devices  21.2 us (4%)
  between operations  14.8 us (3%)
  starting transfers between devices  9.31 us (2%)
    gather x1, local copies, waits for them, and re-layouts, on_device(): slab.reshape(count_items, planes, length * wide)[:, :, placed_sites]  42.6 us
    psum x1, blocking collectives, on_device(): projected = lax.psum(projected, 'ga')  38.1 us
    scatter x1, local copies, waits for them, and re-layouts, on_device(): placed = jnp.zeros((count_items, planes, length * wide), jnp.float32).at[...  37 us
    gather x2, local copies, waits for them, and re-layouts, on_device(): jnp.take(field, line_index, axis=1)  24.6 us
    scatter-add x1, other arithmetic, on_device(): out_field = (field * doubled_potential).at[:, line_index].add(spread)  24.2 us
    dot_general x2, matrix products, along_inner(): return jnp.matmul(slab, table, precision=highest)  23.8 us
    unnamed x29, local copies, waits for them, and re-layouts  21.6 us
    dot_general x2, matrix products, along_outer(): mixed = jnp.einsum('qx,pxk->pqk', stacked, slab, precision=highest)  18 us
  transfers between devices with their start and end apart: 3, of which 2 were waited for; matrix products, arithmetic and copies ran while one was open for 67% of the time, Pallas kernels for 0%

commit v1 on v0

v1 whole, which is shorter than its diff:
```python
import math

import jax
import jax.numpy as jnp
import numpy as np
from jax import lax
from jax.experimental import pallas as pl
from jax.experimental.pallas import tpu as pltpu
from jax.sharding import PartitionSpec as P

N = 160
HALF = N // 2
N_GA = 8
PLANES = N // N_GA
NCOL = 5120
COLS = NCOL // N_GA
SLOTS = 192
ROWS_X = N + 8
LIMIT = 60 * 1024 * 1024
bf16 = jnp.bfloat16
f32 = jnp.float32


def split_np(matrix):
    high = np.asarray(matrix, np.float32).astype(jnp.bfloat16)
    low = (np.asarray(matrix, np.float64) - high.astype(np.float64)).astype(np.float32).astype(jnp.bfloat16)
    return high, low


def fourier(orient):
    index = np.arange(N)
    angle = (np.outer(index, index) % N) * (2.0 * np.pi / N)
    return np.cos(angle), orient * np.sin(angle)


def stage_matrix(orient, paired):
    cosine, sine = fourier(orient)
    if paired:
        order = np.concatenate([np.arange(0, N, 2), np.arange(1, N, 2)])
        cosine, sine = cosine[:, order], sine[:, order]
    ch, cl = split_np(cosine)
    sh, sl = split_np(sine)
    return np.concatenate([ch, sh, ch, sh, cl, sl], axis=1)


def sent_order():
    rows = []
    for d in range(N_GA):
        for part, span in ((0, range(16)), (1, range(16)), (0, range(16, 20)), (1, range(16, 20))):
            rows += [(part, d * PLANES + p) for p in span]
    return rows


def depth_matrices():
    cosine, sine = fourier(1.0)
    full = np.block([[cosine, -sine], [sine, cosine]])
    back = np.block([[cosine, sine], [-sine, cosine]]) / float(N**3)
    order = np.array([part * N + z for part, z in sent_order()])
    return full[order].astype(np.float32), back[:, order].astype(np.float32)


def lanes():
    return lax.broadcasted_iota(jnp.int32, (1, 128), 1)


def fourier_rows(matrix, blocks):
    lane = lanes()
    sign = jnp.where(lane < 64, -1.0, 1.0).astype(f32)
    pieces = []
    for block in blocks:
        turned = pltpu.roll(block, 64, 1) * sign
        high = block.astype(bf16)
        low = (block - high.astype(f32)).astype(bf16)
        turned_high = turned.astype(bf16)
        turned_low = (turned - turned_high.astype(f32)).astype(bf16)
        pieces.append(jnp.concatenate([high, turned_high, low, turned_low, high, turned_high], axis=0))
    right = pieces[0] if len(pieces) == 1 else jnp.concatenate(pieces, axis=1)
    return jnp.dot(matrix, right, preferred_element_type=f32)


def exchange_pairs(first, second):
    odd = (lanes() // 32) % 2 == 1
    even_rows = jnp.where(odd, pltpu.roll(second, 32, 1), first)
    odd_rows = jnp.where(odd, second, pltpu.roll(first, 96, 1))
    return jnp.concatenate([even_rows, odd_rows], axis=0)


def forward_kernel(
    site_row, box_row, recv, first_matrix, second_matrix, potential, beta, applied, partial, grid, mixed, stage, sums
):
    def transpose(t, carry):
        d = t // 5
        start = pl.multiple_of((t % 5) * 128, 128)
        block = recv[d, :, pl.ds(start, 128)]
        real, imag, rest = block[0:16], block[16:32], block[32:40]
        swapped = pltpu.roll(rest, 4, 0)
        zero = jnp.zeros((8, 128), f32)
        stacked = jnp.concatenate(
            [real, rest, zero, real, rest, zero, imag, swapped, zero, imag, swapped, zero], axis=0
        )
        stage[pl.ds(pl.multiple_of(t * 128, 128), 128), :] = stacked.T
        return carry

    lax.fori_loop(0, NCOL // 128, transpose, 0)

    def clear(t, carry):
        grid[pl.ds(pl.multiple_of(t * 256, 256), 256), :] = jnp.zeros((256, 128), f32)
        return carry

    lax.fori_loop(0, N * N // 256, clear, 0)

    def place(t, carry):
        base = t * 16
        for k in range(16):
            grid[pl.ds(site_row[base + k], 1), :] = stage[pl.ds(base + k, 1), :]
        return carry

    lax.fori_loop(0, NCOL // 16, place, 0)

    odd = (lanes() // 32) % 2 == 1

    def along_x(t, carry):
        blocks = []
        for k in range(2):
            start = pl.multiple_of((t * 2 + k) * 2 * N, 16)
            even_y = grid[pl.ds(start, N), :]
            odd_y = grid[pl.ds(start + N, N), :]
            blocks.append(jnp.where(odd, odd_y, even_y))
        result = fourier_rows(first_matrix[...], blocks)
        for k in range(2):
            mixed[t * 2 + k] = result[:, k * 128 : (k + 1) * 128]
        return carry

    lax.fori_loop(0, HALF // 2, along_x, 0)

    def along_y(t, carry):
        blocks = []
        for k in range(2):
            pair = t * 2 + k
            blocks.append(exchange_pairs(mixed[:, 2 * pair, :], mixed[:, 2 * pair + 1, :]))
        result = fourier_rows(second_matrix[...], blocks)
        for k in range(2):
            pair = t * 2 + k
            values = result[:, k * 128 : (k + 1) * 128]
            start = pl.multiple_of(pair * ROWS_X, 8)
            grid[pl.ds(start, N), :] = values
            grid[pl.ds(start + N, 8), :] = values[0:8]
            applied[pl.ds(start, N), :] = values * potential[pl.ds(pl.multiple_of(pair * N, 16), N), :]
            applied[pl.ds(start + N, 8), :] = jnp.zeros((8, 128), f32)
        return carry

    lax.fori_loop(0, HALF // 2, along_y, 0)

    def project(t, carry):
        for k in range(4):
            s = t * 4 + k
            total = jnp.zeros((8, 128), f32)
            for i in range(5):
                weight = beta[pl.ds(pl.multiple_of(s * 40 + i * 8, 8), 8), :]
                total = total + weight * grid[pl.ds(box_row[s * 5 + i], 8), :]
            sums[pl.ds(pl.multiple_of(s * 8, 8), 8), :] = total
        return carry

    lax.fori_loop(0, SLOTS // 4, project, 0)
    totals = jnp.sum(sums[...].reshape(SLOTS, 8, 128), axis=1)
    row = lax.broadcasted_iota(jnp.int32, (8, 128), 0)
    column = lax.broadcasted_iota(jnp.int32, (8, 128), 1)
    chooser = jnp.where(row == column // 64, 1.0, 0.0).astype(f32)
    partial[...] = lax.dot_general(
        chooser, totals, (((1,), (1,)), ((), ())), precision=lax.Precision.HIGHEST, preferred_element_type=f32
    )


def backward_kernel(
    site_row, box_row, weights, applied_in, beta, first_matrix, second_matrix, parity, sent, applied, mixed, grid, stage
):
    lane = lanes()

    def add_boxes(s, carry):
        weight = jnp.where(lane < 64, weights[0, s], weights[1, s])
        for i in range(5):
            start = box_row[s * 5 + i]
            extra = beta[pl.ds(pl.multiple_of(s * 40 + i * 8, 8), 8), :] * weight
            applied[pl.ds(start, 8), :] = applied[pl.ds(start, 8), :] + extra
        return carry

    applied[...] = applied_in[...]
    lax.fori_loop(0, SLOTS, add_boxes, 0)

    def along_y(t, carry):
        blocks = []
        for k in range(2):
            start = pl.multiple_of((t * 2 + k) * ROWS_X, 8)
            top = applied[pl.ds(start, 8), :] + applied[pl.ds(start + N, 8), :]
            blocks.append(jnp.concatenate([top, applied[pl.ds(start + 8, N - 8), :]], axis=0))
        result = fourier_rows(first_matrix[...], blocks)
        for k in range(2):
            mixed[t * 2 + k] = result[:, k * 128 : (k + 1) * 128]
        return carry

    lax.fori_loop(0, HALF // 2, along_y, 0)

    def along_x(t, carry):
        blocks = []
        for k in range(2):
            pair = t * 2 + k
            blocks.append(exchange_pairs(mixed[:, 2 * pair, :], mixed[:, 2 * pair + 1, :]))
        result = fourier_rows(second_matrix[...], blocks)
        for k in range(2):
            grid[pl.ds(pl.multiple_of((t * 2 + k) * N, 16), N), :] = result[:, k * 128 : (k + 1) * 128]
        return carry

    lax.fori_loop(0, HALF // 2, along_x, 0)

    def pick(t, carry):
        base = t * 16
        for k in range(16):
            stage[pl.ds(base + k, 1), :] = grid[pl.ds(site_row[base + k], 1), :]
        return carry

    lax.fori_loop(0, NCOL // 16, pick, 0)

    def transpose(t, carry):
        d = t // 5
        start = pl.multiple_of((t % 5) * 128, 128)
        turned = stage[pl.ds(pl.multiple_of(t * 128, 128), 128), :].T
        is_odd = parity[pl.ds(t, 1), :] > 0
        real = jnp.where(is_odd, turned[32:56], turned[0:24])
        imag = jnp.where(is_odd, turned[96:120], turned[64:88])
        upper = lax.broadcasted_iota(jnp.int32, (8, 128), 0) < 4
        rest = jnp.where(upper, real[16:24], pltpu.roll(imag[16:24], 4, 0))
        sent[d, :, pl.ds(start, 128)] = jnp.concatenate([real[0:16], imag[0:16], rest], axis=0)
        return carry

    lax.fori_loop(0, NCOL // 128, transpose, 0)


def whole(space=pltpu.VMEM):
    return pl.BlockSpec(memory_space=space)


def frequency(index):
    return jnp.where(index < HALF, index, index - N).astype(f32)


def box_tables(box_cells, box_atom, box_beta):
    corner = box_cells[:, 0]
    plane = corner // (N * N)
    row = corner // N % N
    col = corner % N
    pair = (row[:, None] // 2 + jnp.arange(5, dtype=jnp.int32)[None, :]) % HALF
    box_row = (pair * ROWS_X + col[:, None]).reshape(-1)
    values = box_beta.reshape(SLOTS, 2, 8, 8)
    even = jnp.pad(values, ((0, 0), (0, 0), (0, 2), (0, 0)))
    shifted = jnp.pad(values, ((0, 0), (0, 0), (1, 1), (0, 0)))
    chosen = jnp.where((row % 2 == 0)[:, None, None, None], even, shifted)
    chosen = chosen.reshape(SLOTS, 2, 5, 2, 8)
    lane = jnp.arange(128, dtype=jnp.int32)
    lane_half = lane // 32 % 2
    lane_plane = lane % 32
    low = jnp.where(lane_half == 0, chosen[:, 0, :, 0, :, None], chosen[:, 0, :, 1, :, None])
    high = jnp.where(lane_half == 0, chosen[:, 1, :, 0, :, None], chosen[:, 1, :, 1, :, None])
    at = plane[:, None, None, None]
    table = jnp.where(lane_plane == at, low, 0.0) + jnp.where(lane_plane == at + 1, high, 0.0)
    return box_row, table.reshape(SLOTS * 40, 128)


def potential_rows(potential):
    turned = potential.reshape(PLANES, HALF, 2, N).transpose(1, 3, 2, 0)
    padded = jnp.pad(turned, ((0, 0), (0, 0), (0, 0), (0, 12))).reshape(HALF * N, 64)
    return jnp.concatenate([padded, padded], axis=1)


def on_device(trial_bands, basis_bands, column_sites, potential, box_cells, box_atom, box_beta, strength):
    forward_depth, backward_depth = depth_matrices()
    trial = trial_bands.reshape(2 * N, COLS)
    high3 = lax.Precision.HIGH
    basis_all = lax.all_gather(basis_bands, "band", axis=0, tiled=True)
    depth = jnp.dot(jnp.asarray(forward_depth), trial, precision=high3).reshape(N_GA, 40, COLS)
    atoms_all = lax.all_gather(box_atom, "ga", axis=0, tiled=True)
    recv = lax.all_to_all(depth, "ga", split_axis=0, concat_axis=0, tiled=True)

    site_x = column_sites // N
    site_y = column_sites % N
    box_row, beta = box_tables(box_cells, box_atom, box_beta)
    pot = potential_rows(potential)
    row_count = HALF * ROWS_X
    applied, partial = pl.pallas_call(
        forward_kernel,
        out_shape=(
            jax.ShapeDtypeStruct((row_count, 128), f32),
            jax.ShapeDtypeStruct((8, SLOTS), f32),
        ),
        in_specs=[whole(pltpu.SMEM), whole(pltpu.SMEM)] + [whole()] * 5,
        out_specs=(whole(), whole()),
        scratch_shapes=[
            pltpu.VMEM((N * N, 128), f32),
            pltpu.VMEM((HALF, N, 128), f32),
            pltpu.VMEM((NCOL, 128), f32),
            pltpu.VMEM((SLOTS * 8, 128), f32),
        ],
        compiler_params=pltpu.CompilerParams(vmem_limit_bytes=LIMIT),
        name="planes_forward",
    )(
        site_y * N + site_x,
        box_row,
        recv,
        jnp.asarray(stage_matrix(1.0, False)),
        jnp.asarray(stage_matrix(1.0, True)),
        pot,
        beta,
    )
    same = (atoms_all[:, None] == box_atom[None, :]).astype(f32) * strength[box_atom][None, :]
    copies = jnp.broadcast_to(partial[None, :2], (N_GA, 2, SLOTS))
    shared = lax.all_to_all(copies, "ga", split_axis=0, concat_axis=0, tiled=True)
    shared = shared.transpose(1, 0, 2).reshape(2, N_GA * SLOTS)
    weights = jnp.dot(shared, same, precision=lax.Precision.HIGHEST)
    sent = pl.pallas_call(
        backward_kernel,
        out_shape=jax.ShapeDtypeStruct((N_GA, 40, COLS), f32),
        in_specs=[whole(pltpu.SMEM)] * 3 + [whole()] * 5,
        out_specs=whole(),
        scratch_shapes=[
            pltpu.VMEM((row_count, 128), f32),
            pltpu.VMEM((HALF, N, 128), f32),
            pltpu.VMEM((HALF * N, 128), f32),
            pltpu.VMEM((NCOL, 128), f32),
        ],
        compiler_params=pltpu.CompilerParams(vmem_limit_bytes=LIMIT),
        name="planes_backward",
    )(
        (site_y // 2) * N + site_x,
        box_row,
        weights,
        applied,
        beta,
        jnp.asarray(stage_matrix(-1.0, False)),
        jnp.asarray(stage_matrix(-1.0, True)),
        (site_y % 2).reshape(NCOL // 128, 128),
    )
    returned = lax.all_to_all(sent, "ga", split_axis=0, concat_axis=0, tiled=True)
    spectrum = jnp.dot(jnp.asarray(backward_depth), returned.reshape(2 * N, COLS), precision=high3)
    own = lax.dynamic_slice_in_dim(column_sites, lax.axis_index("ga") * COLS, COLS)
    fz = frequency(jnp.arange(N, dtype=jnp.int32))
    kinetic = (2.0 / float(N * N)) * (
        fz[:, None] ** 2 + frequency(own // N)[None, :] ** 2 + frequency(own % N)[None, :] ** 2
    )
    result = spectrum.reshape(2, N, COLS) + kinetic * trial.reshape(2, N, COLS)
    real_sum = jnp.sum(basis_all * result[None], axis=(1, 2, 3))
    imag_sum = jnp.sum(basis_all[:, 0] * result[None, 1] - basis_all[:, 1] * result[None, 0], axis=(1, 2))
    partial_gram = jnp.stack([real_sum, imag_sum]) * (1.0 / math.sqrt(N * NCOL))
    copies = jnp.broadcast_to(partial_gram[None], (N_GA, 2, 16))
    gram = jnp.sum(lax.all_to_all(copies, "ga", split_axis=0, concat_axis=0, tiled=True), axis=0)
    return (result[None], gram[:, :, None])


def solution(mesh):
    placed = (
        P("band", None, None, "ga"),
        P("band", None, None, "ga"),
        P(),
        P("ga", None, None),
        P("ga", None),
        P("ga"),
        P("ga", None),
        P(),
    )
    return jax.shard_map(
        on_device,
        mesh=mesh,
        in_specs=placed,
        out_specs=(P("band", None, None, "ga"), P(None, None, "band")),
        check_vma=False,
    )
```

time: 488 us -> 224 us (0.46); the launches traced: 481 us -> 224 us
  local copies, waits for them, and re-layouts: 210 us -> 25.8 us
  matrix products: 117 us -> 5.41 us
  Pallas kernels: 0 us -> 104 us
  blocking collectives: 55.5 us -> 21.3 us
  other arithmetic: 53.6 us -> 26.8 us
  waiting for transfers between devices: 21.2 us -> 10.7 us
  starting transfers between devices: 9.31 us -> 14.8 us
    dot_general x18 -> x3, matrix products: 117 us -> 5.41 us  [the longest x1 3.05 us: on_device(): jnp.dot(jnp.asarray(forward_depth), trial, precision=high3)]
    pallas_call x0 -> x2, Pallas kernels: none -> 104 us  [the longest x1 52.9 us: on_device(): pl.pallas_call(forward_kernel, out_shape=(jax.ShapeDtypeStruct((row_count...]
    gather x4 -> x1, local copies, waits for them, and re-layouts: 68.6 us -> 1.17 us  [on_device(): strength[box_atom][None, :]]
    psum x2 -> x0, blocking collectives: 55.5 us -> none  [the longest x1 38.1 us: on_device(): projected = lax.psum(projected, 'ga')]
    scatter x1 -> x0, local copies, waits for them, and re-layouts: 37 us -> none  [on_device(): placed = jnp.zeros((count_items, planes, length * wide), jnp.float32).at[...]
    reshape x4 -> x5, local copies, waits for them, and re-layouts: 50.2 us -> 14 us  [the longest x2 9.56 us: potential_rows(): jnp.pad(turned, ((0, 0), (0, 0), (0, 0), (0, 12))).reshape(HALF * N, 64)]
    scatter-add x2 -> x0, other arithmetic: 25.5 us -> none  [the longest x1 24.2 us: on_device(): out_field = (field * doubled_potential).at[:, line_index].add(spread)]
    unnamed x29 -> x24, local copies, waits for them, and re-layouts: 21.6 us -> 2.98 us
  transfers between devices with their start and end apart: 3 -> 4, of which waited for: 2 -> 1; matrix products, arithmetic and copies ran while one was open for 67% -> 21% of each run, Pallas kernels for 0% -> 46%
where the time goes in v1:
time: 224 us
  Pallas kernels  104 us (46%)
  other arithmetic  26.8 us (12%)
  local copies, waits for them, and re-layouts  25.8 us (12%)
  blocking collectives  21.3 us (10%)
  between operations  15 us (7%)
  starting transfers between devices  14.8 us (7%)
  waiting for transfers between devices  10.7 us (5%)
  matrix products  5.41 us (2%)
    pallas_call x1, Pallas kernels, on_device(): pl.pallas_call(forward_kernel, out_shape=(jax.ShapeDtypeStruct((row_count...  52.9 us
    pallas_call x1, Pallas kernels, on_device(): pl.pallas_call(backward_kernel, out_shape=jax.ShapeDtypeStruct((N_GA, 40,...  50.9 us
    unnamed x1, blocking collectives  12.6 us
    all_to_all x1, waiting for transfers between devices, on_device(): lax.all_to_all(sent, 'ga', split_axis=0, concat_axis=0, tiled=True)  9.97 us
    reshape x2, local copies, waits for them, and re-layouts, potential_rows(): jnp.pad(turned, ((0, 0), (0, 0), (0, 0), (0, 12))).reshape(HALF * N, 64)  9.56 us
    all_to_all x1, blocking collectives, on_device(): lax.all_to_all(copies, 'ga', split_axis=0, concat_axis=0, tiled=True)  8.71 us
    concatenate x1, other arithmetic, potential_rows(): return jnp.concatenate([padded, padded], axis=1)  8.27 us
    reduce_sum x1, other arithmetic, on_device(): real_sum = jnp.sum(basis_all * result[None], axis=(1, 2, 3))  6.76 us
  transfers between devices with their start and end apart: 4, of which 1 were waited for; matrix products, arithmetic and copies ran while one was open for 21% of the time, Pallas kernels for 46%

profile of v1, /device:TPU:0, one launch (start us, length us, event | category | flops | bytes accessed | tf_op | source)
XLA Modules:
  0.0 223.7 jit_solution(13019330899572893068)
XLA Ops:
  7.2 0.7 all-gather.2.cloned.1.call-update
  7.9 3.0 %fusion.45 = f32[8,40,640]{2,1,0:T(8,128)} fusion(f32[8,40,320]{2,1,0:T(8,128)} %constant.187, f32[320,640,1]{1,0,2:T(8,128)} %bitcast.67), kind=kOutput, calls=%fused_computation.110 | convolution fusion | flops 393216000 | bytes 2048000 | tf_op jit(solution)/shard_map/dot_general | solution.py:279
  11.0 5.4 %all-to-all-start = ((f32[8,40,640]{2,1,0:T(8,128)}), f32[8,40,640]{2,1,0:T(8,128)}, u32[]{:S(2)}, u32[]{:S(2)}) async-start(f32[8,40,640]{2,1,0:T(8,128)} %fusion.45), calls=%async_computation | async-start | bytes 1638400 | tf_op jit(solution)/shard_map/all_to_all | solution.py:281
  16.5 3.9 %reshape.300 = f32[20,80,2,160]{3,2,1,0:T(2,128)S(1)} reshape(f32[20,160,160]{2,1,0:T(8,128)} %param.17) | data formatting | bytes 4096000 | tf_op jit(solution)/shard_map/reshape | solution.py:269
  20.8 2.9 %pad.12 = f32[80,160,2,32]{1,0,3,2:T(8,128)} pad(f32[80,160,2,20]{1,0,3,2:T(8,128)S(1)} %bitcast.66, f32[]{:T(128)} %constant.159.clone.1), padding=0_0x0_0x0_0x0_12 | pad | bytes 5324804 | tf_op jit(solution)/shard_map/jit(_pad)/pad | solution.py:270
  23.8 5.5 %reshape.301 = f32[12800,64]{0,1:T(8,128)S(1)} reshape(f32[80,160,2,32]{1,0,3,2:T(8,128)} %pad.12) | data formatting | bytes 6553600 | tf_op jit(solution)/shard_map/reshape | solution.py:270
  29.3 4.1 %copy.52 = f32[12800,64]{1,0:T(8,128)} copy(f32[12800,64]{0,1:T(8,128)S(1)} %reshape.301) | data formatting | bytes 6553600 | tf_op jit(solution)/shard_map/reshape | solution.py:270
  34.3 8.3 %pad_maximum_fusion.potential = f32[12800,128]{1,0:T(8,128)} fusion(f32[12800,64]{1,0:T(8,128)} %copy.52), kind=kLoop, calls=%fused_computation.8 | loop fusion | flops 1638400 | bytes 9830400 | tf_op jit(solution)/shard_map/concatenate | solution.py:271
  45.2 6.1 %select_add_fusion.beta = f32[7680,128]{1,0:T(8,128)} fusion(f32[7680]{0:T(1024)S(1)} %broadcast_in_dim.118, f32[7680]{0:T(1024)S(1)} %broadcast_in_dim.116, f32[7680]{0:T(1024)S(1)} %broadcast_in_dim.111, f32[7680]{0:T(1024)S(1)} %broadcast_in_dim.109, pred[192,128]{1,0:T(8,128)(4,1)S(1)} %get-tuple-element.38, pred[128]{0:T(512)(128)(4,1)S(1)} %fusion.39, ...), kind=kLoop, calls=%fused_computation.9 | loop fusion | flops 4915200 | bytes 4104320 | tf_op jit(solution)/shard_map/add | solution.py:264
  52.6 52.9 %planes_forward.1 = (f32[13440,128]{1,0:T(8,128)}, f32[8,192]{1,0:T(8,128)}) custom-call(s32[5120]{0:T(1024)} %get-tuple-element.35.site_row, s32[960]{0:T(1024)} %fusion.28.box_row, f32[8,40,640]{2,1,0:T(8,128)} %all-to-all-done.recv, bf16[160,960]{1,0:T(8,128)(2,1)} %constant.173.clone.first_matrix, bf16[160,960]{1,0:T(8,128)(2,1)} %constant.174.clone.second_matrix, ...), custom_call_target="tpu_custom_call" | custom-call | tf_op jit(solution)/shard_map/planes_forward/pallas_call | solution.py:288
  105.6 0.7 slice.35
  106.9 5.7 %all-to-all-start.1 = ((f32[8,2,192]{2,1,0:T(2,128)}), f32[8,2,192]{2,1,0:T(2,128)S(1)}, u32[]{:S(2)}, u32[]{:S(2)}) async-start(f32[8,2,192]{2,1,0:T(2,128)} %broadcast_in_dim.120), calls=%async_computation.1 | async-start | bytes 32768 | tf_op jit(solution)/shard_map/all_to_all | solution.py:315
  114.2 1.2 gather_fusion
  115.3 12.6 %all-reduce.3 = s32[1536]{0:T(1024)S(1)} all-reduce(s32[1536]{0:T(1024)S(1)} %dynamic-update-slice), channel_id=1, replica_groups=mesh['band'=16,'ga'=8] {'ga'}, use_global_device_ids=true, to_apply=%add.3 | all-reduce | flops 1536 | bytes 12288
  128.0 1.5 fusion.4.weights
  129.5 50.9 %planes_backward.1 = f32[8,40,640]{2,1,0:T(8,128)} custom-call(s32[5120]{0:T(1024)} %get-tuple-element.36.site_row, s32[960]{0:T(1024)} %fusion.28.box_row, f32[2,192]{1,0:T(2,128)} %fusion.4.weights, f32[13440,128]{1,0:T(8,128)} %get-tuple-element.5.applied_in, f32[7680,128]{1,0:T(8,128)} %select_add_fusion.beta, ...), custom_call_target="tpu_custom_call" | custom-call | tf_op jit(solution)/shard_map/planes_backward/pallas_call | solution.py:318
  180.4 3.7 %all-to-all-start.2 = ((f32[8,40,640]{2,1,0:T(8,128)}), f32[8,40,640]{2,1,0:T(8,128)S(1)}, u32[]{:S(2)}, u32[]{:S(2)}) async-start(f32[8,40,640]{2,1,0:T(8,128)} %planes_backward.1), calls=%async_computation.2 | async-start | bytes 1638400 | tf_op jit(solution)/shard_map/all_to_all | solution.py:341
  184.3 10.0 %all-to-all-done.2 = f32[8,40,640]{2,1,0:T(8,128)S(1)} async-done(((f32[8,40,640]{2,1,0:T(8,128)}), f32[8,40,640]{2,1,0:T(8,128)S(1)}, u32[]{:S(2)}, u32[]{:S(2)}) %all-to-all-start.2) | async-done | bytes 819232 | tf_op jit(solution)/shard_map/all_to_all | solution.py:341
  194.3 0.9 fusion.46
  195.3 0.8 slice_bitcast_fusion.3
  196.3 6.8 %multiply_reduce_fusion = f32[16]{0:T(128)S(1)} fusion(f32[16,2,160,640]{3,2,1,0:T(8,128)} %all-gather.2.cloned.1.call-done, f32[2,160,640]{2,1,0:T(8,128)S(1)} %bitcast.71), kind=kLoop, calls=%fused_computation.1 | loop fusion | flops 6553584 | bytes 13926464 | tf_op jit(solution)/shard_map/reduce_sum | solution.py:349
  203.0 2.0 copy-done.1
  205.0 2.5 %fusion.2 = f32[16]{0:T(128)S(1)} fusion(f32[16,2,160,640]{3,2,1,0:T(8,128)S(1)} %copy-done.1, f32[160,640]{1,0:T(8,128)} %get-tuple-element.27, f32[160,640]{1,0:T(8,128)S(1)} %get-tuple-element.26), kind=kLoop, calls=%fused_computation.5 | loop fusion | flops 6553584 | bytes 13926464 | tf_op jit(solution)/shard_map/reduce_sum | solution.py:350
  207.5 8.7 %all_to_all.20 = f32[8,2,16]{2,1,0:T(2,128)S(1)} all-to-all(f32[8,2,16]{2,1,0:T(2,128)S(1)} %broadcast_in_dim.122), channel_id=1, replica_groups=mesh['band'=16,'ga'=8] {'ga'}, dimensions={0} | all-to-all | bytes 2048 | tf_op jit(solution)/shard_map/all_to_all | solution.py:353
  (65 shorter events, 8.0 us)
Async XLA Ops:
  7.2 107.0 %copy-start = (f32[1024]{0:T(1024)S(1)}, f32[1024]{0:T(1024)}, u32[]{:S(2)}) copy-start(f32[1024]{0:T(1024)} %param.21) | copy-start | bytes 12292
  7.2 9.2 %copy-start.6 = (f32[192,128]{1,0:T(8,128)S(1)}, f32[192,128]{1,0:T(8,128)}, u32[]{:S(2)}) copy-start(f32[192,128]{1,0:T(8,128)} %param.20) | copy-start | bytes 294916
  7.2 189.1 %all-gather.2.cloned.1.call-start = ((), (), s32[]{:S(2)}) async-start(), calls=%async_computation.4 | async-start | bytes 13926400 | tf_op jit(solution)/shard_map/all_gather | solution.py:278
  11.0 41.7 %all-to-all-start = ((f32[8,40,640]{2,1,0:T(8,128)}), f32[8,40,640]{2,1,0:T(8,128)}, u32[]{:S(2)}, u32[]{:S(2)}) async-start(f32[8,40,640]{2,1,0:T(8,128)} %fusion.45), calls=%async_computation | async-start | bytes 1638400 | tf_op jit(solution)/shard_map/all_to_all | solution.py:281
  29.3 4.1 %copy-start.4 = (s32[192,128]{1,0:T(8,128)S(1)}, s32[192,128]{1,0:T(8,128)}, u32[]{:S(2)}) copy-start(s32[192,128]{1,0:T(8,128)} %param.18) | copy-start | bytes 294916
  43.7 7.7 %copy-start.8 = (s32[192]{0:T(256)S(1)}, s32[192]{0:T(256)}, u32[]{:S(2)}) copy-start(s32[192]{0:T(256)} %param.19) | copy-start | bytes 2308
  43.7 8.3 %copy-start.7 = (s32[5120]{0:T(1024)S(1)}, s32[5120]{0:T(1024)}, u32[]{:S(2)}) copy-start(s32[5120]{0:T(1024)} %param.16) | copy-start | bytes 61444
  52.6 60.0 %copy-start.9 = (u32[128]{0:T(128)S(1)}, u32[128]{0:T(128)}, u32[]{:S(2)}) copy-start(u32[128]{0:T(128)} %constant.190) | copy-start | bytes 1540
  106.9 21.1 %all-to-all-start.1 = ((f32[8,2,192]{2,1,0:T(2,128)}), f32[8,2,192]{2,1,0:T(2,128)S(1)}, u32[]{:S(2)}, u32[]{:S(2)}) async-start(f32[8,2,192]{2,1,0:T(2,128)} %broadcast_in_dim.120), calls=%async_computation.1 | async-start | bytes 32768 | tf_op jit(solution)/shard_map/all_to_all | solution.py:315
  129.5 64.8 %copy-start.5 = (f32[320,320]{1,0:T(8,128)S(1)}, f32[320,320]{1,0:T(8,128)}, u32[]{:S(2)}) copy-start(f32[320,320]{1,0:T(8,128)} %constant.177.clone) | copy-start | bytes 1228804
  180.4 14.8 %copy-start.2 = (f32[1,2,160,640]{3,2,1,0:T(8,128)S(1)}, f32[1,2,160,640]{3,2,1,0:T(8,128)}, u32[]{:S(2)}) copy-start(f32[1,2,160,640]{3,2,1,0:T(8,128)} %param.14) | copy-start | bytes 2457604
  180.4 13.9 %all-to-all-start.2 = ((f32[8,40,640]{2,1,0:T(8,128)}), f32[8,40,640]{2,1,0:T(8,128)S(1)}, u32[]{:S(2)}, u32[]{:S(2)}) async-start(f32[8,40,640]{2,1,0:T(8,128)} %planes_backward.1), calls=%async_computation.2 | async-start | bytes 1638400 | tf_op jit(solution)/shard_map/all_to_all | solution.py:341
  196.2 6.8 %copy-start.3 = (f32[1,2,160,640]{3,2,1,0:T(8,128)}, f32[1,2,160,640]{3,2,1,0:T(8,128)S(1)}, u32[]{:S(2)}) copy-start(f32[1,2,160,640]{3,2,1,0:T(8,128)S(1)} %multiply_add_fusion) | copy-start | bytes 2457604
  196.3 8.7 %copy-start.1 = (f32[16,2,160,640]{3,2,1,0:T(8,128)S(1)}, f32[16,2,160,640]{3,2,1,0:T(8,128)}, u32[]{:S(2)}) copy-start(f32[16,2,160,640]{3,2,1,0:T(8,128)} %all-gather.2.cloned.1.call-done) | copy-start | bytes 39321604
Sparse Core Ops, SparseCore 0:
  10.5 98.3 all-gather.1

commit v2 on v1

v2 whole, which is shorter than its diff:
```python
import math

import jax
import jax.numpy as jnp
import numpy as np
from jax import lax
from jax.experimental import pallas as pl
from jax.experimental.pallas import tpu as pltpu
from jax.sharding import PartitionSpec as P

N = 160
HALF = N // 2
N_GA = 8
PLANES = N // N_GA
NCOL = 5120
COLS = NCOL // N_GA
SLOTS = 192
ROWS_X = N + 8
ATOMS = 1024
GROUP = 40
PITCH = 164
LIMIT = 60 * 1024 * 1024
bf16 = jnp.bfloat16
f32 = jnp.float32


def split_np(matrix):
    high = np.asarray(matrix, np.float32).astype(jnp.bfloat16)
    low = (np.asarray(matrix, np.float64) - high.astype(np.float64)).astype(np.float32).astype(jnp.bfloat16)
    return high, low


def fourier(orient):
    index = np.arange(N)
    angle = (np.outer(index, index) % N) * (2.0 * np.pi / N)
    return np.cos(angle), orient * np.sin(angle)


def stage_matrix(orient, paired):
    cosine, sine = fourier(orient)
    if paired:
        order = np.concatenate([np.arange(0, N, 2), np.arange(1, N, 2)])
        cosine, sine = cosine[:, order], sine[:, order]
    ch, cl = split_np(cosine)
    sh, sl = split_np(sine)
    return np.concatenate([ch, sh, ch, sh, cl, sl], axis=1)


def sent_order():
    rows = []
    for d in range(N_GA):
        for part, span in ((0, range(16)), (1, range(16)), (0, range(16, 20)), (1, range(16, 20))):
            rows += [(part, d * PLANES + p) for p in span]
    return rows


def depth_matrices():
    cosine, sine = fourier(1.0)
    full = np.block([[cosine, -sine], [sine, cosine]])
    back = np.block([[cosine, sine], [-sine, cosine]]) / float(N**3)
    order = np.array([part * N + z for part, z in sent_order()])
    tables = []
    for matrix in (full[order], back[:, order]):
        high, low = split_np(matrix)
        tables.append(np.concatenate([high, high, low], axis=1))
    return tables


def lanes():
    return lax.broadcasted_iota(jnp.int32, (1, 128), 1)


def fourier_rows(matrix, blocks):
    lane = lanes()
    sign = jnp.where(lane < 64, -1.0, 1.0).astype(f32)
    pieces = []
    for block in blocks:
        turned = pltpu.roll(block, 64, 1) * sign
        high = block.astype(bf16)
        low = (block - high.astype(f32)).astype(bf16)
        turned_high = turned.astype(bf16)
        turned_low = (turned - turned_high.astype(f32)).astype(bf16)
        pieces.append(jnp.concatenate([high, turned_high, low, turned_low, high, turned_high], axis=0))
    right = pieces[0] if len(pieces) == 1 else jnp.concatenate(pieces, axis=1)
    return jnp.dot(matrix, right, preferred_element_type=f32)


def exchange_pairs(first, second):
    odd = (lanes() // 32) % 2 == 1
    even_rows = jnp.where(odd, pltpu.roll(second, 32, 1), first)
    odd_rows = jnp.where(odd, second, pltpu.roll(first, 96, 1))
    return jnp.concatenate([even_rows, odd_rows], axis=0)


def split3(values):
    high = values.astype(bf16)
    rest = values - high.astype(f32)
    middle = rest.astype(bf16)
    return high, middle, (rest - middle.astype(f32)).astype(bf16)


def exact_dot(first, second, contract):
    total = None
    if isinstance(first, tuple):
        terms = [(piece, second) for piece in first]
    else:
        terms = [(first, piece) for piece in second]
    for left, right in terms:
        product = lax.dot_general(left, right, (contract, ((), ())), preferred_element_type=f32)
        total = product if total is None else total + product
    return total


def atom_table(atoms):
    row = lax.broadcasted_iota(jnp.int32, (ATOMS, SLOTS), 0)
    return jnp.where(atoms[...] == row, 1.0, 0.0).astype(bf16)


def box_places(box_base, s):
    places = []
    for i in range(5):
        start = box_base[s] + i * ROWS_X
        places.append(pl.ds(jnp.where(start >= HALF * ROWS_X, start - HALF * ROWS_X, start), 8))
    return places


def depth_product(matrix, values):
    high = values.astype(bf16)
    low = (values - high.astype(f32)).astype(bf16)
    return jnp.dot(matrix, jnp.concatenate([high, low, high], axis=0), preferred_element_type=f32)


def depth_kernel(matrix, values, out):
    out[...] = depth_product(matrix[...], values[...])


def prepare_kernel(
    box_plane, box_odd, potential, box_beta, potential_out, beta_out, rows, table, sems
):
    copies = []

    def send(source, target, start, size):
        span = pl.ds(start, size)
        copies.append(pltpu.make_async_copy(source.at[span], target.at[span], sems.at[len(copies)]))
        copies[-1].start()

    lane = lanes()
    lane_odd = (lane // 32) % 2 == 1
    lane_plane = lane % 32
    local_box = lax.broadcasted_iota(jnp.int32, (16, 128), 0) % 8
    local_plane = lane_plane - lax.broadcasted_iota(jnp.int32, (16, 128), 0) // 8
    nothing = jnp.zeros((8, 128), f32)

    def spread(t, carry):
        values = box_beta[pl.ds(pl.multiple_of(t * 8, 8), 8), :]
        both = jnp.concatenate([values, pltpu.roll(values, 64, 1)], axis=0)
        high = both.astype(bf16).astype(f32)
        left = jnp.concatenate([high, both - high], axis=0).T[0:64].astype(bf16)
        masks = []
        for k in range(8):
            hit = (local_box == k) & (local_plane == box_plane[t * 8 + k])
            masks.append(jnp.where(hit, 1.0, 0.0))
        mask = jnp.concatenate(masks, axis=1)
        right = jnp.concatenate([mask, mask], axis=0).astype(bf16)
        lines = jnp.dot(left, right, preferred_element_type=f32)
        for k in range(8):
            s = t * 8 + k
            shifted = box_odd[s] > 0
            line = [lines[x * 8 : x * 8 + 8, k * 128 : (k + 1) * 128] for x in range(8)]
            for i in range(5):
                even = line[2 * i] if i < 4 else nothing
                straight = jnp.where(lane_odd, line[2 * i + 1], even) if i < 4 else nothing
                moved = jnp.where(lane_odd, even, line[2 * i - 1] if i > 0 else nothing)
                table[pl.ds(pl.multiple_of(s * 40 + i * 8, 8), 8), :] = jnp.where(shifted, moved, straight)
        return carry

    def spread_two(t, carry):
        spread(2 * t, 0)
        spread(2 * t + 1, 0)
        return carry

    for piece in range(2):
        lax.fori_loop(piece * 6, piece * 6 + 6, spread_two, 0)
        send(table, beta_out, piece * SLOTS * 20, SLOTS * 20)
    zero = jnp.zeros((8, N), f32)
    for piece in range(4):
        for k in range(HALF // 4):
            pair = piece * (HALF // 4) + k
            pieces = []
            for half in range(2):
                plane = potential[:, 2 * pair + half, :]
                pieces += [plane[0:8], plane[8:16], jnp.concatenate([plane[16:20], zero[0:4]], axis=0), zero]
            stacked = jnp.concatenate(pieces + pieces, axis=0)
            rows[pair * N : pair * N + 128, :] = stacked[:, 0:128].T
            rows[pair * N + 128 : pair * N + N, :] = stacked[:, 128:N].T
        send(rows, potential_out, piece * (HALF // 4) * N, (HALF // 4) * N)
    for copy in copies:
        copy.wait()


def finish_kernel(
    matrix, returned, trial, plane_kinetic, basis_all, result, gram, basis, sums, sems
):
    pairs = basis_all.shape[0] // 2

    def brought(m):
        span = pl.ds(2 * m, 2)
        return pltpu.make_async_copy(basis_all.at[span], basis.at[span], sems.at[m])

    for m in range(pairs):
        brought(m).start()
    depth = lax.broadcasted_iota(jnp.int32, (N, 1), 0)
    depth = jnp.where(depth < HALF, depth, depth - N).astype(f32)
    kinetic = (2.0 / float(N * N)) * (depth * depth) + plane_kinetic[...]
    spectrum = depth_product(matrix[...], returned[...])
    result[0:N, :] = spectrum[0:N] + kinetic * trial[0:N, :]
    result[N : 2 * N, :] = spectrum[N : 2 * N] + kinetic * trial[N : 2 * N, :]

    def one_pair(m, carry):
        brought(m).wait()

        def rows(t, totals):
            totals = list(totals)
            for k in range(4):
                real_at = pl.ds(pl.multiple_of(t * 32 + k * 8, 8), 8)
                imag_at = pl.ds(pl.multiple_of(N + t * 32 + k * 8, 8), 8)
                real, imag = result[real_at, :], result[imag_at, :]
                for n in range(2):
                    left_real, left_imag = basis[2 * m + n, real_at, :], basis[2 * m + n, imag_at, :]
                    totals[2 * n] = totals[2 * n] + (left_real * real + left_imag * imag)
                    totals[2 * n + 1] = totals[2 * n + 1] + (left_real * imag - left_imag * real)
            return tuple(totals)

        totals = lax.fori_loop(0, N // 32, rows, (jnp.zeros((8, COLS), f32),) * 4)
        for n, total in enumerate(totals):
            line = jnp.sum(total, axis=0, keepdims=True)
            short = line[:, 0:128]
            for j in range(1, COLS // 128):
                short = short + line[:, j * 128 : (j + 1) * 128]
            sums[pl.ds(m * 4 + n, 1), :] = short
        return carry

    lax.fori_loop(0, pairs, one_pair, 0)
    gram[...] = exact_dot(jnp.ones((8, 128), bf16), split3(sums[...]), ((1,), (1,)))


def forward_kernel(
    site_row, box_base, recv, first_matrix, second_matrix, atoms, potential_in, beta_in,
    applied_out, shared, grid, mixed, stage, sums, applied, potential, beta, sems,
):
    potential_copy = pltpu.make_async_copy(potential_in, potential, sems.at[0])
    beta_copy = pltpu.make_async_copy(beta_in, beta, sems.at[1])
    potential_copy.start()
    beta_copy.start()

    def transpose(d, carry):
        for j in range(COLS // 128):
            block = recv[d, :, j * 128 : (j + 1) * 128]
            real, imag, rest = block[0:16], block[16:32], block[32:40]
            swapped = pltpu.roll(rest, 4, 0)
            zero = jnp.zeros((8, 128), f32)
            stacked = jnp.concatenate(
                [real, rest, zero, real, rest, zero, imag, swapped, zero, imag, swapped, zero], axis=0
            )
            stage[pl.ds(pl.multiple_of(d * COLS + j * 128, 128), 128), :] = stacked.T
        return carry

    lax.fori_loop(0, N_GA, transpose, 0)

    def clear(t, carry):
        grid[pl.ds(pl.multiple_of(t * 256, 256), 256), :] = jnp.zeros((256, 128), f32)
        return carry

    lax.fori_loop(0, N * N // 256, clear, 0)

    def place(t, carry):
        base = t * 64
        for k in range(64):
            grid[pl.ds(site_row[base + k], 1), :] = stage[pl.ds(base + k, 1), :]
        return carry

    lax.fori_loop(0, NCOL // 64, place, 0)

    odd = (lanes() // 32) % 2 == 1

    def along_x(t, carry):
        blocks = []
        for k in range(GROUP):
            start = pl.multiple_of((t * GROUP + k) * 2 * N, 16)
            even_y = grid[pl.ds(start, N), :]
            odd_y = grid[pl.ds(start + N, N), :]
            blocks.append(jnp.where(odd, odd_y, even_y))
        result = fourier_rows(first_matrix[...], blocks)
        for k in range(GROUP):
            mixed[pl.ds((t * GROUP + k) * PITCH, N), :] = result[:, k * 128 : (k + 1) * 128]
        return carry

    lax.fori_loop(0, HALF // GROUP, along_x, 0)
    potential_copy.wait()

    def along_y(t, carry):
        blocks = []
        for k in range(GROUP):
            pair = t * GROUP + k
            blocks.append(
                exchange_pairs(
                    mixed[pl.ds(2 * pair, HALF, stride=PITCH), :], mixed[pl.ds(2 * pair + 1, HALF, stride=PITCH), :]
                )
            )
        result = fourier_rows(second_matrix[...], blocks)
        for k in range(GROUP):
            pair = t * GROUP + k
            values = result[:, k * 128 : (k + 1) * 128]
            start = pl.multiple_of(pair * ROWS_X, 8)
            grid[pl.ds(start, N), :] = values
            grid[pl.ds(start + N, 8), :] = values[0:8]
            applied[pl.ds(start, N), :] = values * potential[pl.ds(pl.multiple_of(pair * N, 16), N), :]
            applied[pl.ds(start + N, 8), :] = jnp.zeros((8, 128), f32)
        return carry

    copies = []
    for t in range(HALF // GROUP):
        along_y(t, 0)
        piece = pl.ds(t * GROUP * ROWS_X, GROUP * ROWS_X)
        copy = pltpu.make_async_copy(applied.at[piece], applied_out.at[piece], sems.at[2 + t])
        copy.start()
        copies.append(copy)
    beta_copy.wait()

    def project(t, carry):
        for k in range(4):
            s = t * 4 + k
            total = jnp.zeros((8, 128), f32)
            for i, place in enumerate(box_places(box_base, s)):
                weight = beta[pl.ds(pl.multiple_of(s * 40 + i * 8, 8), 8), :]
                total = total + weight * grid[place, :]
            sums[pl.ds(pl.multiple_of(s * 8, 8), 8), :] = total
        return carry

    lax.fori_loop(0, SLOTS // 4, project, 0)
    totals = jnp.sum(sums[...].reshape(SLOTS, 8, 128), axis=1)
    row = lax.broadcasted_iota(jnp.int32, (8, 128), 0)
    column = lax.broadcasted_iota(jnp.int32, (8, 128), 1)
    chooser = jnp.where(row == column // 64, 1.0, 0.0).astype(bf16)
    partial = exact_dot(chooser, split3(totals), ((1,), (1,)))
    by_atom = exact_dot(split3(partial), atom_table(atoms), ((1,), (1,)))
    for part in range(2):
        for r in range(4):
            values = by_atom[part : part + 1, r * 256 : (r + 1) * 256]
            for d in range(N_GA):
                shared[d, part * 4 + r : part * 4 + r + 1, :] = values
    for copy in copies:
        copy.wait()


def backward_kernel(
    site_row, box_base, shared, strength, atoms, first_matrix, second_matrix, parity, applied_in, beta_in,
    sent, applied, mixed, grid, stage, beta, weights, sems,
):
    applied_copy = pltpu.make_async_copy(applied_in, applied, sems.at[0])
    beta_copy = pltpu.make_async_copy(beta_in, beta, sems.at[1])
    applied_copy.start()
    beta_copy.start()
    total = jnp.sum(shared[...], axis=0)
    by_part = []
    for part in range(2):
        whole_row = jnp.concatenate([total[part * 4 + r : part * 4 + r + 1, :] for r in range(4)], axis=1)
        by_part.append(jnp.broadcast_to(whole_row * strength[...], (64, ATOMS)))
    spread = jnp.concatenate(by_part, axis=0)
    weights[...] = exact_dot(split3(spread), atom_table(atoms), ((1,), (0,))).T
    applied_copy.wait()
    beta_copy.wait()

    def add_boxes(t, carry):
        for k in range(2):
            s = t * 2 + k
            weight = weights[pl.ds(s, 1), :]
            places = box_places(box_base, s)
            olds = [applied[place, :] for place in places]
            for i in range(5):
                applied[places[i], :] = olds[i] + beta[pl.ds(pl.multiple_of(s * 40 + i * 8, 8), 8), :] * weight
        return carry

    lax.fori_loop(0, SLOTS // 2, add_boxes, 0)

    def along_y(t, carry):
        blocks = []
        for k in range(GROUP):
            start = pl.multiple_of((t * GROUP + k) * ROWS_X, 8)
            top = applied[pl.ds(start, 8), :] + applied[pl.ds(start + N, 8), :]
            blocks.append(jnp.concatenate([top, applied[pl.ds(start + 8, N - 8), :]], axis=0))
        result = fourier_rows(first_matrix[...], blocks)
        for k in range(GROUP):
            mixed[pl.ds((t * GROUP + k) * PITCH, N), :] = result[:, k * 128 : (k + 1) * 128]
        return carry

    lax.fori_loop(0, HALF // GROUP, along_y, 0)

    def along_x(t, carry):
        blocks = []
        for k in range(GROUP):
            pair = t * GROUP + k
            blocks.append(
                exchange_pairs(
                    mixed[pl.ds(2 * pair, HALF, stride=PITCH), :], mixed[pl.ds(2 * pair + 1, HALF, stride=PITCH), :]
                )
            )
        result = fourier_rows(second_matrix[...], blocks)
        for k in range(GROUP):
            grid[pl.ds(pl.multiple_of((t * GROUP + k) * N, 16), N), :] = result[:, k * 128 : (k + 1) * 128]
        return carry

    lax.fori_loop(0, HALF // GROUP, along_x, 0)

    def pick(t, carry):
        base = t * 64
        for k in range(64):
            stage[pl.ds(base + k, 1), :] = grid[pl.ds(site_row[base + k], 1), :]
        return carry

    lax.fori_loop(0, NCOL // 64, pick, 0)
    upper = lax.broadcasted_iota(jnp.int32, (8, 128), 0) < 4

    def transpose(d, carry):
        for j in range(COLS // 128):
            turned = stage[pl.ds(pl.multiple_of(d * COLS + j * 128, 128), 128), :].T
            is_odd = parity[pl.ds(d * (COLS // 128) + j, 1), :] > 0
            real = jnp.where(is_odd, turned[32:56], turned[0:24])
            imag = jnp.where(is_odd, turned[96:120], turned[64:88])
            rest = jnp.where(upper, real[16:24], pltpu.roll(imag[16:24], 4, 0))
            sent[d, :, j * 128 : (j + 1) * 128] = jnp.concatenate([real[0:16], imag[0:16], rest], axis=0)
        return carry

    lax.fori_loop(0, N_GA, transpose, 0)


def whole(space=pltpu.VMEM):
    return pl.BlockSpec(memory_space=space)


def frequency(index):
    return jnp.where(index < HALF, index, index - N).astype(f32)


def on_device(trial_bands, basis_bands, column_sites, potential, box_cells, box_atom, box_beta, strength):
    forward_depth, backward_depth = depth_matrices()
    bands = lax.axis_size("band")
    basis_all = lax.all_gather(basis_bands.reshape(2 * N, COLS), "band", axis=0)
    trial = trial_bands.reshape(2 * N, COLS)
    depth = pl.pallas_call(
        depth_kernel,
        out_shape=jax.ShapeDtypeStruct((2 * N, COLS), f32),
        in_specs=[whole()] * 2,
        out_specs=whole(),
        compiler_params=pltpu.CompilerParams(vmem_limit_bytes=LIMIT),
        name="depth",
    )(jnp.asarray(forward_depth), trial)
    recv = lax.all_to_all(depth.reshape(N_GA, 40, COLS), "ga", split_axis=0, concat_axis=0, tiled=True)

    site_x = column_sites // N
    site_y = column_sites - site_x * N
    corner = box_cells[:, 0]
    corner_plane = corner // (N * N)
    in_plane = corner - corner_plane * (N * N)
    corner_x = in_plane // N
    box_base = (corner_x // 2) * ROWS_X + (in_plane - corner_x * N)
    pot, beta = pl.pallas_call(
        prepare_kernel,
        out_shape=(
            jax.ShapeDtypeStruct((HALF * N, 128), f32),
            jax.ShapeDtypeStruct((SLOTS * 40, 128), f32),
        ),
        in_specs=[whole(pltpu.SMEM)] * 2 + [whole()] * 2,
        out_specs=(whole(pl.ANY), whole(pl.ANY)),
        scratch_shapes=[
            pltpu.VMEM((HALF * N, 128), f32),
            pltpu.VMEM((SLOTS * 40, 128), f32),
            pltpu.SemaphoreType.DMA((6,)),
        ],
        compiler_params=pltpu.CompilerParams(vmem_limit_bytes=LIMIT),
        cost_estimate=pl.CostEstimate(flops=0, bytes_accessed=14000000, transcendentals=0),
        name="prepare",
    )(corner_plane, corner_x % 2, potential, box_beta)
    row_count = HALF * ROWS_X
    applied, shared = pl.pallas_call(
        forward_kernel,
        out_shape=(
            jax.ShapeDtypeStruct((row_count, 128), f32),
            jax.ShapeDtypeStruct((N_GA, 8, ATOMS // 4), f32),
        ),
        in_specs=[whole(pltpu.SMEM)] * 2 + [whole()] * 4 + [whole(pl.ANY)] * 2,
        out_specs=(whole(pl.ANY), whole()),
        scratch_shapes=[
            pltpu.VMEM((N * N, 128), f32),
            pltpu.VMEM((HALF * PITCH, 128), f32),
            pltpu.VMEM((NCOL, 128), f32),
            pltpu.VMEM((SLOTS * 8, 128), f32),
            pltpu.VMEM((row_count, 128), f32),
            pltpu.VMEM((HALF * N, 128), f32),
            pltpu.VMEM((SLOTS * 40, 128), f32),
            pltpu.SemaphoreType.DMA((2 + HALF // GROUP,)),
        ],
        compiler_params=pltpu.CompilerParams(vmem_limit_bytes=LIMIT),
        name="planes_forward",
    )(
        site_y * N + site_x,
        box_base,
        recv,
        jnp.asarray(stage_matrix(1.0, False)),
        jnp.asarray(stage_matrix(1.0, True)),
        box_atom.reshape(1, SLOTS),
        pot,
        beta,
    )
    shared = lax.all_to_all(shared, "ga", split_axis=0, concat_axis=0, tiled=True)
    sent = pl.pallas_call(
        backward_kernel,
        out_shape=jax.ShapeDtypeStruct((N_GA, 40, COLS), f32),
        in_specs=[whole(pltpu.SMEM)] * 2 + [whole()] * 6 + [whole(pl.ANY)] * 2,
        out_specs=whole(),
        scratch_shapes=[
            pltpu.VMEM((row_count, 128), f32),
            pltpu.VMEM((HALF * PITCH, 128), f32),
            pltpu.VMEM((HALF * N, 128), f32),
            pltpu.VMEM((NCOL, 128), f32),
            pltpu.VMEM((SLOTS * 40, 128), f32),
            pltpu.VMEM((SLOTS, 128), f32),
            pltpu.SemaphoreType.DMA((2,)),
        ],
        compiler_params=pltpu.CompilerParams(vmem_limit_bytes=LIMIT),
        name="planes_backward",
    )(
        (site_y // 2) * N + site_x,
        box_base,
        shared,
        strength.reshape(1, ATOMS),
        box_atom.reshape(1, SLOTS),
        jnp.asarray(stage_matrix(-1.0, False)),
        jnp.asarray(stage_matrix(-1.0, True)),
        (site_y % 2).reshape(NCOL // 128, 128),
        applied,
        beta,
    )
    returned = lax.all_to_all(sent, "ga", split_axis=0, concat_axis=0, tiled=True)
    own = lax.dynamic_slice_in_dim(column_sites, lax.axis_index("ga") * COLS, COLS)
    plane_kinetic = (2.0 / float(N * N)) * (frequency(own // N) ** 2 + frequency(own % N) ** 2)
    result, gram = pl.pallas_call(
        finish_kernel,
        out_shape=(
            jax.ShapeDtypeStruct((2 * N, COLS), f32),
            jax.ShapeDtypeStruct((8, 2 * bands), f32),
        ),
        in_specs=[whole()] * 4 + [whole(pl.ANY)],
        out_specs=(whole(), whole()),
        scratch_shapes=[
            pltpu.VMEM((bands, 2 * N, COLS), f32),
            pltpu.VMEM((2 * bands, 128), f32),
            pltpu.SemaphoreType.DMA((bands // 2,)),
        ],
        compiler_params=pltpu.CompilerParams(vmem_limit_bytes=LIMIT),
        name="finish",
    )(
        jnp.asarray(backward_depth),
        returned.reshape(2 * N, COLS),
        trial,
        plane_kinetic.reshape(1, COLS),
        basis_all,
    )
    gram = lax.all_to_all(gram, "ga", split_axis=0, concat_axis=0, tiled=True)
    gram = (jnp.sum(gram, axis=0) * (1.0 / math.sqrt(N * NCOL))).reshape(bands, 2).T
    return (result.reshape(trial_bands.shape), gram[:, :, None])


def solution(mesh):
    placed = (
        P("band", None, None, "ga"),
        P("band", None, None, "ga"),
        P(),
        P("ga", None, None),
        P("ga", None),
        P("ga"),
        P("ga", None),
        P(),
    )
    return jax.shard_map(
        on_device,
        mesh=mesh,
        in_specs=placed,
        out_specs=(P("band", None, None, "ga"), P(None, None, "band")),
        check_vma=False,
    )
```

time: 224 us -> 143 us (0.64)
  Pallas kernels: 104 us -> 63.5 us
  other arithmetic: 26.8 us -> 2.59 us
  local copies, waits for them, and re-layouts: 25.8 us -> 3.22 us
  waiting for transfers between devices: 10.7 us -> 22.8 us
  blocking collectives: 21.3 us -> 27.8 us
  starting transfers between devices: 14.8 us -> 9 us
  matrix products: 5.41 us -> 0 us
    pallas_call x1, Pallas kernels: 52.9 us -> 20.3 us  [on_device(): pl.pallas_call(forward_kernel, out_shape=(jax.ShapeDtypeStruct((row_count...]
    pallas_call x1, Pallas kernels: 50.9 us -> 22.5 us  [on_device(): pl.pallas_call(backward_kernel, out_shape=jax.ShapeDtypeStruct((N_GA, 40,...]
    pallas_call x0 -> x3, Pallas kernels: none -> 20.7 us  [the longest x1 10.1 us: on_device(): pl.pallas_call(prepare_kernel, out_shape=(jax.ShapeDtypeStruct((HALF * N,...]
    all_to_all x1 -> x2, blocking collectives: 8.71 us -> 27.8 us  [the longest x1 15.6 us: on_device(): gram = lax.all_to_all(gram, 'ga', split_axis=0, concat_axis=0, tiled=True)]
    reshape x5 -> x1, local copies, waits for them, and re-layouts: 14 us -> 0.58 us  [on_device(): plane_kinetic.reshape(1, COLS)]
    unnamed x1 -> x0, blocking collectives: 12.6 us -> none
    all_gather x1, waiting for transfers between devices: 0.02 us -> 10.7 us  [on_device(): basis_all = lax.all_gather(basis_bands.reshape(2 * N, COLS), 'band', axis=0)]
    reduce_sum x3 -> x1, other arithmetic: 9.85 us -> 0.03 us  [on_device(): jnp.sum(gram, axis=0) * (1.0 / math.sqrt(N * NCOL))]
  transfers between devices with their start and end apart: 4 -> 3, of which waited for: 1 -> 2; matrix products, arithmetic and copies ran while one was open for 21% -> 3% of each run, Pallas kernels for 46% -> 39%
where the time goes in v2:
time: 143 us
  Pallas kernels  63.5 us (44%)
  blocking collectives  27.8 us (19%)
  waiting for transfers between devices  22.8 us (16%)
  between operations  14.1 us (10%)
  starting transfers between devices  9 us (6%)
  local copies, waits for them, and re-layouts  3.22 us (2%)
  other arithmetic  2.59 us (2%)
    pallas_call x1, Pallas kernels, on_device(): pl.pallas_call(backward_kernel, out_shape=jax.ShapeDtypeStruct((N_GA, 40,...  22.5 us
    pallas_call x1, Pallas kernels, on_device(): pl.pallas_call(forward_kernel, out_shape=(jax.ShapeDtypeStruct((row_count...  20.3 us
    all_to_all x1, blocking collectives, on_device(): gram = lax.all_to_all(gram, 'ga', split_axis=0, concat_axis=0, tiled=True)  15.6 us
    all_to_all x1, blocking collectives, on_device(): lax.all_to_all(shared, 'ga', split_axis=0, concat_axis=0, tiled=True)  12.2 us
    all_to_all x1, waiting for transfers between devices, on_device(): lax.all_to_all(sent, 'ga', split_axis=0, concat_axis=0, tiled=True)  11.4 us
    all_gather x1, waiting for transfers between devices, on_device(): basis_all = lax.all_gather(basis_bands.reshape(2 * N, COLS), 'band', axis=0)  10.7 us
    pallas_call x1, Pallas kernels, on_device(): pl.pallas_call(prepare_kernel, out_shape=(jax.ShapeDtypeStruct((HALF * N,...  10.1 us
    pallas_call x1, Pallas kernels, on_device(): pl.pallas_call(finish_kernel, out_shape=(jax.ShapeDtypeStruct((2 * N, COL...  7.6 us
  transfers between devices with their start and end apart: 3, of which 2 were waited for; matrix products, arithmetic and copies ran while one was open for 3% of the time, Pallas kernels for 39%

profile of v2, /device:TPU:0, one launch (start us, length us, event | category | flops | bytes accessed | tf_op | source)
XLA Modules:
  0.0 142.9 jit_solution(12241134832170568952)
XLA Ops:
  7.2 0.0 copy-start.2
  7.2 0.0 all-gather.2.cloned.1.call-start
  7.2 0.7 all-gather.2.cloned.1.call-update
  7.9 2.9 %depth.1 = f32[320,640]{1,0:T(8,128)} custom-call(bf16[320,960]{1,0:T(8,128)(2,1)} %constant.110.clone.matrix, f32[320,640]{1,0:T(8,128)} %bitcast.16), custom_call_target="tpu_custom_call" | custom-call | tf_op jit(solution)/shard_map/depth/pallas_call | solution.py:450
  10.8 5.4 %all-to-all-start = ((f32[8,40,640]{2,1,0:T(8,128)}), f32[8,40,640]{2,1,0:T(8,128)S(1)}, u32[]{:S(2)}, u32[]{:S(2)}) async-start(f32[8,40,640]{2,1,0:T(8,128)} %bitcast.15), calls=%async_computation | async-start | bytes 1638400 | tf_op jit(solution)/shard_map/all_to_all | solution.py:458
  16.2 1.0 slice_reduce_fusion
  17.2 0.6 and_select_fusion
  17.8 10.1 %prepare.1 = (f32[12800,128]{1,0:T(8,128)}, f32[7680,128]{1,0:T(8,128)}) custom-call(s32[192]{0:T(256)} %get-tuple-element.22.box_plane, s32[192]{0:T(256)} %get-tuple-element.20.box_odd, f32[20,160,160]{2,1,0:T(8,128)} %potential.1, f32[192,128]{1,0:T(8,128)} %box_beta.1), custom_call_target="tpu_custom_call" | custom-call | bytes 14000000 | tf_op jit(solution)/shard_map/prepare/pallas_call | solution.py:467
  28.0 1.2 subtract_add_fusion.box_base
  29.2 0.7 fusion.2
  29.9 0.0 all-to-all-done.recv
  29.9 0.9 copy-done
  30.8 20.3 %planes_forward.1 = (f32[13440,128]{1,0:T(8,128)}, f32[8,8,256]{2,1,0:T(8,128)}) custom-call(s32[5120]{0:T(1024)} %get-tuple-element.24.site_row, s32[192]{0:T(256)} %subtract_add_fusion.box_base, f32[8,40,640]{2,1,0:T(8,128)} %copy-done, bf16[160,960]{1,0:T(8,128)(2,1)} %constant.111.clone.first_matrix, bf16[160,960]{1,0:T(8,128)(2,1)} %constant.112.clone.second_matrix, ...), custom_call_target="tpu_custom_call" | custom-call | tf_op jit(solution)/shard_map/planes_forward/pallas_call | solution.py:485
  51.1 12.2 %all_to_all.24.shared = f32[8,8,256]{2,1,0:T(8,128)} all-to-all(f32[8,8,256]{2,1,0:T(8,128)} %get-tuple-element.10), channel_id=1, replica_groups=mesh['band'=16,'ga'=8] {'ga'}, dimensions={0} | all-to-all | bytes 131072 | tf_op jit(solution)/shard_map/all_to_all | solution.py:515
  63.2 22.5 %planes_backward.1 = f32[8,40,640]{2,1,0:T(8,128)} custom-call(s32[5120]{0:T(1024)} %get-tuple-element.25.site_row, s32[192]{0:T(256)} %subtract_add_fusion.box_base, f32[8,8,256]{2,1,0:T(8,128)} %all_to_all.24.shared, f32[1,1024]{1,0:T(1,128)} %bitcast.21, s32[1,192]{1,0:T(1,128)} %bitcast.23, bf16[160,960]{1,0:T(8,128)(2,1)} %constant.113.clone.first_matrix, ...), custom_call_target="tpu_custom_call" | custom-call | tf_op jit(solution)/shard_map/planes_backward/pallas_call | solution.py:516
  85.8 3.6 %all-to-all-start.2 = ((f32[8,40,640]{2,1,0:T(8,128)}), f32[8,40,640]{2,1,0:T(8,128)S(1)}, u32[]{:S(2)}, u32[]{:S(2)}) async-start(f32[8,40,640]{2,1,0:T(8,128)} %planes_backward.1), calls=%async_computation.2 | async-start | bytes 1638400 | tf_op jit(solution)/shard_map/all_to_all | solution.py:544
  89.3 0.1 fusion.8
  89.4 0.6 reshape.41.plane_kinetic
  90.0 11.4 %all-to-all-done.2 = f32[8,40,640]{2,1,0:T(8,128)S(1)} async-done(((f32[8,40,640]{2,1,0:T(8,128)}), f32[8,40,640]{2,1,0:T(8,128)S(1)}, u32[]{:S(2)}, u32[]{:S(2)}) %all-to-all-start.2) | async-done | bytes 819232 | tf_op jit(solution)/shard_map/all_to_all | solution.py:544
  101.4 10.7 %all-gather.2.cloned.1.call-done.basis_all = f32[16,320,640]{2,1,0:T(8,128)} async-done(((f32[1,320,640]{2,1,0:T(8,128)}), f32[16,320,640]{2,1,0:T(8,128)}) %all-gather.2.cloned.1.call-update) | async-done | bytes 13107216 | tf_op jit(solution)/shard_map/all_gather | solution.py:448
  112.1 7.6 %finish.1 = (f32[320,640]{1,0:T(8,128)}, f32[8,32]{1,0:T(8,128)}) custom-call(bf16[320,960]{1,0:T(8,128)(2,1)} %constant.115.clone.matrix, f32[320,640]{1,0:T(8,128)} %bitcast.18, f32[320,640]{1,0:T(8,128)} %bitcast.17, f32[1,640]{1,0:T(1,128)} %reshape.41.plane_kinetic, f32[16,320,640]{2,1,0:T(8,128)} %all-gather.2.cloned.1.call-done.basis_all), custom_call_target="tpu_custom_call" | custom-call | tf_op jit(solution)/shard_map/finish/pallas_call | solution.py:547
  119.7 15.6 %all_to_all.25 = f32[8,1,32]{2,1,0:T(1,128)S(1)} all-to-all(f32[8,1,32]{2,1,0:T(1,128)} %bitcast.24), channel_id=1, replica_groups=mesh['band'=16,'ga'=8] {'ga'}, dimensions={0} | all-to-all | bytes 2048 | tf_op jit(solution)/shard_map/all_to_all | solution.py:569
  135.4 0.1 mul.54
  135.5 0.7 copy.22
  (6 shorter events, 0.0 us)
Async XLA Ops:
  7.2 22.0 %copy-start.2 = (s32[5120]{0:T(1024)S(1)}, s32[5120]{0:T(1024)}, u32[]{:S(2)}) copy-start(s32[5120]{0:T(1024)} %param.16) | copy-start | bytes 61444
  7.2 105.0 %all-gather.2.cloned.1.call-start = ((), (), s32[]{:S(2)}) async-start(), calls=%async_computation.4 | async-start | bytes 13926400 | tf_op jit(solution)/shard_map/all_gather | solution.py:448
  10.8 19.0 %all-to-all-start = ((f32[8,40,640]{2,1,0:T(8,128)}), f32[8,40,640]{2,1,0:T(8,128)S(1)}, u32[]{:S(2)}, u32[]{:S(2)}) async-start(f32[8,40,640]{2,1,0:T(8,128)} %bitcast.15), calls=%async_computation | async-start | bytes 1638400 | tf_op jit(solution)/shard_map/all_to_all | solution.py:458
  29.9 0.9 copy-start
  85.8 15.6 %all-to-all-start.2 = ((f32[8,40,640]{2,1,0:T(8,128)}), f32[8,40,640]{2,1,0:T(8,128)S(1)}, u32[]{:S(2)}, u32[]{:S(2)}) async-start(f32[8,40,640]{2,1,0:T(8,128)} %planes_backward.1), calls=%async_computation.2 | async-start | bytes 1638400 | tf_op jit(solution)/shard_map/all_to_all | solution.py:544
  101.4 10.7 %copy-start.1 = (f32[8,40,640]{2,1,0:T(8,128)}, f32[8,40,640]{2,1,0:T(8,128)S(1)}, u32[]{:S(2)}) copy-start(f32[8,40,640]{2,1,0:T(8,128)S(1)} %all-to-all-done.2) | copy-start | bytes 2457604
Sparse Core Ops, SparseCore 0:
  10.5 101.6 all-gather.1

commit v3 on v2

--- a/solution.py
+++ b/solution.py
@@ -198,50 +198,62 @@
         copy.wait()
 
 
-def finish_kernel(
-    matrix, returned, trial, plane_kinetic, basis_all, result, gram, basis, sums, sems
-):
-    pairs = basis_all.shape[0] // 2
-
-    def brought(m):
-        span = pl.ds(2 * m, 2)
-        return pltpu.make_async_copy(basis_all.at[span], basis.at[span], sems.at[m])
-
-    for m in range(pairs):
-        brought(m).start()
+def finish_kernel(core, matrix, returned, trial, plane_kinetic, result, away):
     depth = lax.broadcasted_iota(jnp.int32, (N, 1), 0)
     depth = jnp.where(depth < HALF, depth, depth - N).astype(f32)
     kinetic = (2.0 / float(N * N)) * (depth * depth) + plane_kinetic[...]
     spectrum = depth_product(matrix[...], returned[...])
-    result[0:N, :] = spectrum[0:N] + kinetic * trial[0:N, :]
-    result[N : 2 * N, :] = spectrum[N : 2 * N] + kinetic * trial[N : 2 * N, :]
-
-    def one_pair(m, carry):
-        brought(m).wait()
+    first = core[0] == 0
+    for part in range(2):
+        rows = slice(part * N, part * N + N)
+        values = spectrum[rows] + kinetic * trial[rows, :]
+        result[rows, :] = values
+        away[part * HALF : part * HALF + HALF, :] = jnp.where(first, values[HALF:N], values[0:HALF])
+
+
+def gram_kernel(core, result, brought, basis_all, gram, basis, own_sums, other_sums, sems):
+    chips = basis_all.shape[0]
+
+    def fetch(m):
+        return pltpu.make_async_copy(basis_all.at[m], basis.at[m], sems.at[m])
+
+    for m in range(chips):
+        fetch(m).start()
+    half = core[0] * HALF
+
+    def one_chip(m, carry):
+        fetch(m).wait()
+        chip = jnp.where(m < chips // 2, 2 * m, 2 * chips - 1 - 2 * m)
 
         def rows(t, totals):
             totals = list(totals)
-            for k in range(4):
-                real_at = pl.ds(pl.multiple_of(t * 32 + k * 8, 8), 8)
-                imag_at = pl.ds(pl.multiple_of(N + t * 32 + k * 8, 8), 8)
-                real, imag = result[real_at, :], result[imag_at, :]
-                for n in range(2):
-                    left_real, left_imag = basis[2 * m + n, real_at, :], basis[2 * m + n, imag_at, :]
-                    totals[2 * n] = totals[2 * n] + (left_real * real + left_imag * imag)
-                    totals[2 * n + 1] = totals[2 * n + 1] + (left_real * imag - left_imag * real)
+            row = pl.multiple_of(t * 8, 8)
+            here = (pl.ds(row, 8), pl.ds(row + HALF, 8))
+            mine = (pl.ds(pl.multiple_of(half + row, 8), 8), pl.ds(pl.multiple_of(half + N + row, 8), 8))
+            for j in range(COLS // 128):
+                tile = slice(j * 128, (j + 1) * 128)
+                rights = [(result[mine[0], tile], result[mine[1], tile]), (brought[here[0], tile], brought[here[1], tile])]
+                for slot in range(2):
+                    left_real, left_imag = basis[m, slot, here[0], tile], basis[m, slot, here[1], tile]
+                    for n, (real, imag) in enumerate(rights):
+                        at = n * 4 + slot * 2
+                        totals[at] = totals[at] + (left_real * real + left_imag * imag)
+                        totals[at + 1] = totals[at + 1] + (left_real * imag - left_imag * real)
             return tuple(totals)
 
-        totals = lax.fori_loop(0, N // 32, rows, (jnp.zeros((8, COLS), f32),) * 4)
-        for n, total in enumerate(totals):
-            line = jnp.sum(total, axis=0, keepdims=True)
-            short = line[:, 0:128]
-            for j in range(1, COLS // 128):
-                short = short + line[:, j * 128 : (j + 1) * 128]
-            sums[pl.ds(m * 4 + n, 1), :] = short
-        return carry
-
-    lax.fori_loop(0, pairs, one_pair, 0)
-    gram[...] = exact_dot(jnp.ones((8, 128), bf16), split3(sums[...]), ((1,), (1,)))
+        totals = lax.fori_loop(0, HALF // 8, rows, (jnp.zeros((8, 128), f32),) * 8)
+        for at in range(4):
+            own_sums[pl.ds(chip * 4 + at, 1), :] = jnp.sum(totals[at], axis=0, keepdims=True)
+            other_sums[pl.ds(chip * 4 + at, 1), :] = jnp.sum(totals[4 + at], axis=0, keepdims=True)
+        return carry
+
+    lax.fori_loop(0, chips, one_chip, 0)
+    ones = jnp.ones((8, 128), bf16)
+    own = exact_dot(ones, split3(own_sums[...]), ((1,), (1,)))
+    other = exact_dot(ones, split3(other_sums[...]), ((1,), (1,)))
+    first = core[0] == 0
+    gram[0:8, :] = jnp.where(first, own, other)
+    gram[8:16, :] = jnp.where(first, other, own)
 
 
 def forward_kernel(
@@ -445,7 +457,16 @@
 def on_device(trial_bands, basis_bands, column_sites, potential, box_cells, box_atom, box_beta, strength):
     forward_depth, backward_depth = depth_matrices()
     bands = lax.axis_size("band")
-    basis_all = lax.all_gather(basis_bands.reshape(2 * N, COLS), "band", axis=0)
+    core = lax.axis_index("band") % 2
+    halves = basis_bands.reshape(2, 2, HALF, COLS)
+    swap = [(i, i ^ 1) for i in range(bands)]
+    kept = jnp.where(core == 0, halves[:, 0], halves[:, 1])
+    given = jnp.where(core == 0, halves[:, 1], halves[:, 0])
+    taken = lax.ppermute(given, "band", swap)
+    block = jnp.where(core == 0, jnp.stack([kept, taken]), jnp.stack([taken, kept])).reshape(2, N, COLS)
+    chip_order = list(range(0, bands // 2, 2)) + list(range(bands // 2 - 1, 0, -2))
+    rings = [[2 * chip + k for chip in chip_order] for k in range(2)]
+    basis_all = lax.all_gather(block, "band", axis=0, axis_index_groups=rings)
     trial = trial_bands.reshape(2 * N, COLS)
     depth = pl.pallas_call(
         depth_kernel,
@@ -544,29 +565,40 @@
     returned = lax.all_to_all(sent, "ga", split_axis=0, concat_axis=0, tiled=True)
     own = lax.dynamic_slice_in_dim(column_sites, lax.axis_index("ga") * COLS, COLS)
     plane_kinetic = (2.0 / float(N * N)) * (frequency(own // N) ** 2 + frequency(own % N) ** 2)
-    result, gram = pl.pallas_call(
+    core_number = core.reshape(1)
+    result, away = pl.pallas_call(
         finish_kernel,
-        out_shape=(
-            jax.ShapeDtypeStruct((2 * N, COLS), f32),
-            jax.ShapeDtypeStruct((8, 2 * bands), f32),
-        ),
-        in_specs=[whole()] * 4 + [whole(pl.ANY)],
+        out_shape=(jax.ShapeDtypeStruct((2 * N, COLS), f32), jax.ShapeDtypeStruct((N, COLS), f32)),
+        in_specs=[whole(pltpu.SMEM)] + [whole()] * 4,
         out_specs=(whole(), whole()),
+        compiler_params=pltpu.CompilerParams(vmem_limit_bytes=LIMIT),
+        name="finish",
+    )(
+        core_number,
+        jnp.asarray(backward_depth),
+        returned.reshape(2 * N, COLS),
+        trial,
+        plane_kinetic.reshape(1, COLS),
+    )
+    brought = lax.ppermute(away, "band", swap)
+    gram = pl.pallas_call(
+        gram_kernel,
+        out_shape=jax.ShapeDtypeStruct((16, 2 * bands), f32),
+        in_specs=[whole(pltpu.SMEM)] + [whole()] * 2 + [whole(pl.ANY)],
+        out_specs=whole(),
         scratch_shapes=[
-            pltpu.VMEM((bands, 2 * N, COLS), f32),
+            pltpu.VMEM((bands // 2, 2, N, COLS), f32),
+            pltpu.VMEM((2 * bands, 128), f32),
             pltpu.VMEM((2 * bands, 128), f32),
             pltpu.SemaphoreType.DMA((bands // 2,)),
         ],
         compiler_params=pltpu.CompilerParams(vmem_limit_bytes=LIMIT),
-        name="finish",
-    )(
-        jnp.asarray(backward_depth),
-        returned.reshape(2 * N, COLS),
-        trial,
-        plane_kinetic.reshape(1, COLS),
-        basis_all,
+        name="gram",
+    )(core_number, result, brought, basis_all)
+    chip_group = [[(2 * chip + k) * N_GA + g for k in range(2) for g in range(N_GA)] for chip in range(bands // 2)]
+    gram = lax.all_to_all(
+        gram, ("band", "ga"), split_axis=0, concat_axis=0, tiled=True, axis_index_groups=chip_group
     )
-    gram = lax.all_to_all(gram, "ga", split_axis=0, concat_axis=0, tiled=True)
     gram = (jnp.sum(gram, axis=0) * (1.0 / math.sqrt(N * NCOL))).reshape(bands, 2).T
     return (result.reshape(trial_bands.shape), gram[:, :, None])
 

time: 143 us -> 135 us (0.944); the launches traced: 143 us -> 133 us
  blocking collectives: 27.8 us -> 20.6 us
  waiting for transfers between devices: 22.8 us -> 15.7 us
  other arithmetic: 2.59 us -> 4.75 us
  Pallas kernels: 63.5 us -> 65 us
    all_gather x1, waiting for transfers between devices: 10.7 us -> 0.01 us  [on_device(): basis_all = lax.all_gather(block, 'band', axis=0, axis_index_groups=rings)]
    all_to_all x1, blocking collectives: 15.6 us -> 9.39 us  [on_device(): lax.all_to_all(gram, ('band', 'ga'), split_axis=0, concat_axis=0, tiled=T...]
    pallas_call x0 -> x1, Pallas kernels: none -> 5.74 us  [on_device(): pl.pallas_call(gram_kernel, out_shape=jax.ShapeDtypeStruct((16, 2 * bands...]
    pallas_call x1, Pallas kernels: 7.6 us -> 3.33 us  [on_device(): pl.pallas_call(finish_kernel, out_shape=(jax.ShapeDtypeStruct((2 * N, COL...]
    ppermute x0 -> x2, waiting for transfers between devices: none -> 3.69 us  [the longest x1 1.95 us: on_device(): brought = lax.ppermute(away, 'band', swap)]
    select_n x0 -> x2, other arithmetic: none -> 2.15 us  [the longest x1 1.19 us: on_device(): kept = jnp.where(core == 0, halves[:, 0], halves[:, 1])]
    unnamed x7 -> x11, local copies, waits for them, and re-layouts: 1.55 us -> 3.21 us
  transfers between devices with their start and end apart: 3 -> 5, of which waited for: 2 -> 4; matrix products, arithmetic and copies ran while one was open for 3% -> 2% of each run, Pallas kernels for 39% -> 44%
where the time goes in v3:
time: 135 us; the launch traced here: 133 us
  Pallas kernels  65 us (48%)
  blocking collectives  20.6 us (15%)
  waiting for transfers between devices  15.7 us (12%)
  between operations  14.1 us (10%)
  starting transfers between devices  9.08 us (7%)
  other arithmetic  4.75 us (4%)
  local copies, waits for them, and re-layouts  3.98 us (3%)
    pallas_call x1, Pallas kernels, on_device(): pl.pallas_call(backward_kernel, out_shape=jax.ShapeDtypeStruct((N_GA, 40,...  22.6 us
    pallas_call x1, Pallas kernels, on_device(): pl.pallas_call(forward_kernel, out_shape=(jax.ShapeDtypeStruct((row_count...  20.3 us
    all_to_all x1, blocking collectives, on_device(): lax.all_to_all(shared, 'ga', split_axis=0, concat_axis=0, tiled=True)  11.2 us
    all_to_all x1, waiting for transfers between devices, on_device(): lax.all_to_all(sent, 'ga', split_axis=0, concat_axis=0, tiled=True)  11.1 us
    pallas_call x1, Pallas kernels, on_device(): pl.pallas_call(prepare_kernel, out_shape=(jax.ShapeDtypeStruct((HALF * N,...  10 us
    all_to_all x1, blocking collectives, on_device(): lax.all_to_all(gram, ('band', 'ga'), split_axis=0, concat_axis=0, tiled=T...  9.39 us
    pallas_call x1, Pallas kernels, on_device(): pl.pallas_call(gram_kernel, out_shape=jax.ShapeDtypeStruct((16, 2 * bands...  5.74 us
    all_to_all x1, starting transfers between devices, on_device(): lax.all_to_all(depth.reshape(N_GA, 40, COLS), 'ga', split_axis=0, concat_...  5.4 us
  transfers between devices with their start and end apart: 5, of which 4 were waited for; matrix products, arithmetic and copies ran while one was open for 2% of the time, Pallas kernels for 44%

profile of v3, /device:TPU:0, one launch (start us, length us, event | category | flops | bytes accessed | tf_op | source)
XLA Modules:
  0.0 133.2 jit_solution(6001025514934500025)
XLA Ops:
  7.2 1.2 fusion
  8.5 1.7 %collective-permute-done.1 = f32[2,80,640]{2,1,0:T(8,128)S(1)} collective-permute-done((f32[2,80,640]{2,1,0:T(8,128)S(1)}, f32[2,80,640]{2,1,0:T(8,128)S(1)}, u32[]{:S(2)}, u32[]{:S(2)}) %collective-permute-start.1) | collective-permute-done | bytes 409632 | tf_op jit(solution)/shard_map/ppermute | solution.py:465
  10.3 1.0 maximum_select_fusion
  11.2 2.9 %depth.1 = f32[320,640]{1,0:T(8,128)} custom-call(bf16[320,960]{1,0:T(8,128)(2,1)} %constant.121.clone.matrix, f32[320,640]{1,0:T(8,128)} %bitcast.32), custom_call_target="tpu_custom_call" | custom-call | tf_op jit(solution)/shard_map/depth/pallas_call | solution.py:471
  14.2 5.4 %all-to-all-start = ((f32[8,40,640]{2,1,0:T(8,128)}), f32[8,40,640]{2,1,0:T(8,128)S(1)}, u32[]{:S(2)}, u32[]{:S(2)}) async-start(f32[8,40,640]{2,1,0:T(8,128)} %bitcast.35), calls=%async_computation | async-start | bytes 1638400 | tf_op jit(solution)/shard_map/all_to_all | solution.py:479
  19.7 0.6 and_select_fusion
  20.3 10.0 %prepare.1 = (f32[12800,128]{1,0:T(8,128)}, f32[7680,128]{1,0:T(8,128)}) custom-call(s32[192]{0:T(256)} %get-tuple-element.22.box_plane, s32[192]{0:T(256)} %get-tuple-element.20.box_odd, f32[20,160,160]{2,1,0:T(8,128)} %potential.1, f32[192,128]{1,0:T(8,128)} %box_beta.1), custom_call_target="tpu_custom_call" | custom-call | bytes 14000000 | tf_op jit(solution)/shard_map/prepare/pallas_call | solution.py:488
  30.3 1.2 subtract_add_fusion.box_base
  31.5 0.7 fusion.3
  32.2 0.9 all-to-all-done.recv
  33.1 0.9 copy-done
  34.0 20.3 %planes_forward.1 = (f32[13440,128]{1,0:T(8,128)}, f32[8,8,256]{2,1,0:T(8,128)}) custom-call(s32[5120]{0:T(1024)} %get-tuple-element.26.site_row, s32[192]{0:T(256)} %subtract_add_fusion.box_base, f32[8,40,640]{2,1,0:T(8,128)} %copy-done, bf16[160,960]{1,0:T(8,128)(2,1)} %constant.122.clone.first_matrix, bf16[160,960]{1,0:T(8,128)(2,1)} %constant.123.clone.second_matrix, ...), custom_call_target="tpu_custom_call" | custom-call | tf_op jit(solution)/shard_map/planes_forward/pallas_call | solution.py:506
  54.3 11.2 %all_to_all.24.shared = f32[8,8,256]{2,1,0:T(8,128)} all-to-all(f32[8,8,256]{2,1,0:T(8,128)} %get-tuple-element.10), channel_id=1, replica_groups=mesh['band'=16,'ga'=8] {'ga'}, dimensions={0} | all-to-all | bytes 131072 | tf_op jit(solution)/shard_map/all_to_all | solution.py:536
  65.6 22.6 %planes_backward.1 = f32[8,40,640]{2,1,0:T(8,128)} custom-call(s32[5120]{0:T(1024)} %get-tuple-element.27.site_row, s32[192]{0:T(256)} %subtract_add_fusion.box_base, f32[8,8,256]{2,1,0:T(8,128)} %all_to_all.24.shared, f32[1,1024]{1,0:T(1,128)} %bitcast.42, s32[1,192]{1,0:T(1,128)} %bitcast.44, bf16[160,960]{1,0:T(8,128)(2,1)} %constant.124.clone.first_matrix, ...), custom_call_target="tpu_custom_call" | custom-call | tf_op jit(solution)/shard_map/planes_backward/pallas_call | solution.py:537
  88.2 3.6 %all-to-all-start.2 = ((f32[8,40,640]{2,1,0:T(8,128)}), f32[8,40,640]{2,1,0:T(8,128)S(1)}, u32[]{:S(2)}, u32[]{:S(2)}) async-start(f32[8,40,640]{2,1,0:T(8,128)} %planes_backward.1), calls=%async_computation.2 | async-start | bytes 1638400 | tf_op jit(solution)/shard_map/all_to_all | solution.py:565
  91.8 0.6 reshape.133.plane_kinetic
  92.4 11.1 %all-to-all-done.2 = f32[8,40,640]{2,1,0:T(8,128)S(1)} async-done(((f32[8,40,640]{2,1,0:T(8,128)}), f32[8,40,640]{2,1,0:T(8,128)S(1)}, u32[]{:S(2)}, u32[]{:S(2)}) %all-to-all-start.2) | async-done | bytes 819232 | tf_op jit(solution)/shard_map/all_to_all | solution.py:565
  103.5 0.9 copy-done.1
  104.4 3.3 %finish.1 = (f32[320,640]{1,0:T(8,128)}, f32[160,640]{1,0:T(8,128)}) custom-call(s32[1]{0:T(128)} %bitcast.core, bf16[320,960]{1,0:T(8,128)(2,1)} %constant.126.clone.matrix, f32[320,640]{1,0:T(8,128)} %bitcast.34, f32[320,640]{1,0:T(8,128)} %bitcast.33, f32[1,640]{1,0:T(1,128)} %reshape.133.plane_kinetic), custom_call_target="tpu_custom_call" | custom-call | tf_op jit(solution)/shard_map/finish/pallas_call | solution.py:569
  107.7 2.0 %collective-permute-done.brought = f32[160,640]{1,0:T(8,128)S(1)} collective-permute-done((f32[160,640]{1,0:T(8,128)}, f32[160,640]{1,0:T(8,128)S(1)}, u32[]{:S(2)}, u32[]{:S(2)}) %collective-permute-start) | collective-permute-done | bytes 409632 | tf_op jit(solution)/shard_map/ppermute | solution.py:583
  109.7 0.7 copy-done.2
  110.4 5.7 %gram.1 = f32[16,32]{1,0:T(8,128)} custom-call(s32[1]{0:T(128)} %bitcast.core, f32[320,640]{1,0:T(8,128)} %get-tuple-element.12.result, f32[160,640]{1,0:T(8,128)} %copy-done.2, f32[8,2,160,640]{3,2,1,0:T(8,128)} %all-gather.2.cloned.1.call-done.basis_all), custom_call_target="tpu_custom_call" | custom-call | tf_op jit(solution)/shard_map/gram/pallas_call | solution.py:584
  116.2 9.4 %all_to_all.25 = f32[16,1,32]{2,1,0:T(1,128)S(1)} all-to-all(f32[16,1,32]{2,1,0:T(1,128)} %bitcast.40), channel_id=1, replica_groups={{0,1,2,3,4,5,6,7,8,9,10,11,12,13,14,15},{16,17,18,19,20,21,22,23,24,25,..., dimensions={0} | all-to-all | bytes 4096 | tf_op jit(solution)/shard_map/all_to_all | solution.py:599
  125.7 0.7 copy.28
  (17 shorter events, 0.5 us)
Async XLA Ops:
  7.2 12.4 %copy-start.3 = (s32[192,128]{1,0:T(8,128)S(1)}, s32[192,128]{1,0:T(8,128)}, u32[]{:S(2)}) copy-start(s32[192,128]{1,0:T(8,128)} %param.18) | copy-start | bytes 294916
  7.2 24.4 %copy-start.4 = (s32[5120]{0:T(1024)S(1)}, s32[5120]{0:T(1024)}, u32[]{:S(2)}) copy-start(s32[5120]{0:T(1024)} %param.16) | copy-start | bytes 61444
  7.2 102.5 %all-gather.2.cloned.1.call-start = ((), (), s32[]{:S(2)}) async-start(), calls=%async_computation.4 | async-start | bytes 7372800 | tf_op jit(solution)/shard_map/all_gather | solution.py:469
  8.4 1.8 %collective-permute-start.1 = (f32[2,80,640]{2,1,0:T(8,128)S(1)}, f32[2,80,640]{2,1,0:T(8,128)S(1)}, u32[]{:S(2)}, u32[]{:S(2)}) collective-permute-start(f32[2,80,640]{2,1,0:T(8,128)S(1)} %get-tuple-element.24), channel_id=1, source_target_pairs={{0,8},{8,0},{16,24},{24,16},{32,40},{40,32},{48,56},{56,48},{64,72... | collective-permute-start | bytes 1228808 | tf_op jit(solution)/shard_map/ppermute | solution.py:465
  14.2 18.9 %all-to-all-start = ((f32[8,40,640]{2,1,0:T(8,128)}), f32[8,40,640]{2,1,0:T(8,128)S(1)}, u32[]{:S(2)}, u32[]{:S(2)}) async-start(f32[8,40,640]{2,1,0:T(8,128)} %bitcast.35), calls=%async_computation | async-start | bytes 1638400 | tf_op jit(solution)/shard_map/all_to_all | solution.py:479
  33.1 0.9 copy-start
  88.2 15.3 %all-to-all-start.2 = ((f32[8,40,640]{2,1,0:T(8,128)}), f32[8,40,640]{2,1,0:T(8,128)S(1)}, u32[]{:S(2)}, u32[]{:S(2)}) async-start(f32[8,40,640]{2,1,0:T(8,128)} %planes_backward.1), calls=%async_computation.2 | async-start | bytes 1638400 | tf_op jit(solution)/shard_map/all_to_all | solution.py:565
  103.5 0.9 copy-start.1
  107.7 2.0 %collective-permute-start = (f32[160,640]{1,0:T(8,128)}, f32[160,640]{1,0:T(8,128)S(1)}, u32[]{:S(2)}, u32[]{:S(2)}) collective-permute-start(f32[160,640]{1,0:T(8,128)} %get-tuple-element.13), channel_id=1, source_target_pairs={{0,8},{8,0},{16,24},{24,16},{32,40},{40,32},{48,56},{56,48},{64,72... | collective-permute-start | bytes 1228808 | tf_op jit(solution)/shard_map/ppermute | solution.py:583
  109.7 0.8 copy-start.2
Sparse Core Ops, SparseCore 0:
  11.4 84.0 all-gather.1

commit v4 on v3

--- a/solution.py
+++ b/solution.py
@@ -20,6 +20,7 @@
 GROUP = 40
 PITCH = 164
 LIMIT = 60 * 1024 * 1024
+KEPT = 8 * 1024 * 1024
 bf16 = jnp.bfloat16
 f32 = jnp.float32
 
@@ -258,7 +259,7 @@
 
 def forward_kernel(
     site_row, box_base, recv, first_matrix, second_matrix, atoms, potential_in, beta_in,
-    applied_out, shared, grid, mixed, stage, sums, applied, potential, beta, sems,
+    applied, shared, grid, mixed, stage, sums, potential, beta, sems,
 ):
     potential_copy = pltpu.make_async_copy(potential_in, potential, sems.at[0])
     beta_copy = pltpu.make_async_copy(beta_in, beta, sems.at[1])
@@ -330,13 +331,8 @@
             applied[pl.ds(start + N, 8), :] = jnp.zeros((8, 128), f32)
         return carry
 
-    copies = []
     for t in range(HALF // GROUP):
         along_y(t, 0)
-        piece = pl.ds(t * GROUP * ROWS_X, GROUP * ROWS_X)
-        copy = pltpu.make_async_copy(applied.at[piece], applied_out.at[piece], sems.at[2 + t])
-        copy.start()
-        copies.append(copy)
     beta_copy.wait()
 
     def project(t, carry):
@@ -361,17 +357,13 @@
             values = by_atom[part : part + 1, r * 256 : (r + 1) * 256]
             for d in range(N_GA):
                 shared[d, part * 4 + r : part * 4 + r + 1, :] = values
-    for copy in copies:
-        copy.wait()
 
 
 def backward_kernel(
     site_row, box_base, shared, strength, atoms, first_matrix, second_matrix, parity, applied_in, beta_in,
     sent, applied, mixed, grid, stage, beta, weights, sems,
 ):
-    applied_copy = pltpu.make_async_copy(applied_in, applied, sems.at[0])
-    beta_copy = pltpu.make_async_copy(beta_in, beta, sems.at[1])
-    applied_copy.start()
+    beta_copy = pltpu.make_async_copy(beta_in, beta, sems.at[0])
     beta_copy.start()
     total = jnp.sum(shared[...], axis=0)
     by_part = []
@@ -380,7 +372,6 @@
         by_part.append(jnp.broadcast_to(whole_row * strength[...], (64, ATOMS)))
     spread = jnp.concatenate(by_part, axis=0)
     weights[...] = exact_dot(split3(spread), atom_table(atoms), ((1,), (0,))).T
-    applied_copy.wait()
     beta_copy.wait()
 
     def add_boxes(t, carry):
@@ -506,22 +497,21 @@
     applied, shared = pl.pallas_call(
         forward_kernel,
         out_shape=(
-            jax.ShapeDtypeStruct((row_count, 128), f32),
+            pltpu.VMEM((row_count, 128), f32),
             jax.ShapeDtypeStruct((N_GA, 8, ATOMS // 4), f32),
         ),
         in_specs=[whole(pltpu.SMEM)] * 2 + [whole()] * 4 + [whole(pl.ANY)] * 2,
-        out_specs=(whole(pl.ANY), whole()),
+        out_specs=(whole(), whole()),
         scratch_shapes=[
             pltpu.VMEM((N * N, 128), f32),
             pltpu.VMEM((HALF * PITCH, 128), f32),
             pltpu.VMEM((NCOL, 128), f32),
             pltpu.VMEM((SLOTS * 8, 128), f32),
-            pltpu.VMEM((row_count, 128), f32),
             pltpu.VMEM((HALF * N, 128), f32),
             pltpu.VMEM((SLOTS * 40, 128), f32),
-            pltpu.SemaphoreType.DMA((2 + HALF // GROUP,)),
+            pltpu.SemaphoreType.DMA((2,)),
         ],
-        compiler_params=pltpu.CompilerParams(vmem_limit_bytes=LIMIT),
+        compiler_params=pltpu.CompilerParams(vmem_limit_bytes=LIMIT - KEPT),
         name="planes_forward",
     )(
         site_y * N + site_x,
@@ -534,21 +524,21 @@
         beta,
     )
     shared = lax.all_to_all(shared, "ga", split_axis=0, concat_axis=0, tiled=True)
-    sent = pl.pallas_call(
+    sent, _ = pl.pallas_call(
         backward_kernel,
-        out_shape=jax.ShapeDtypeStruct((N_GA, 40, COLS), f32),
-        in_specs=[whole(pltpu.SMEM)] * 2 + [whole()] * 6 + [whole(pl.ANY)] * 2,
-        out_specs=whole(),
+        out_shape=(jax.ShapeDtypeStruct((N_GA, 40, COLS), f32), pltpu.VMEM((row_count, 128), f32)),
+        in_specs=[whole(pltpu.SMEM)] * 2 + [whole()] * 7 + [whole(pl.ANY)],
+        out_specs=(whole(), whole()),
+        input_output_aliases={8: 1},
         scratch_shapes=[
-            pltpu.VMEM((row_count, 128), f32),
             pltpu.VMEM((HALF * PITCH, 128), f32),
             pltpu.VMEM((HALF * N, 128), f32),
             pltpu.VMEM((NCOL, 128), f32),
             pltpu.VMEM((SLOTS * 40, 128), f32),
             pltpu.VMEM((SLOTS, 128), f32),
-            pltpu.SemaphoreType.DMA((2,)),
+            pltpu.SemaphoreType.DMA((1,)),
         ],
-        compiler_params=pltpu.CompilerParams(vmem_limit_bytes=LIMIT),
+        compiler_params=pltpu.CompilerParams(vmem_limit_bytes=LIMIT - KEPT),
         name="planes_backward",
     )(
         (site_y // 2) * N + site_x,

time: 135 us -> 134 us (level)
  Pallas kernels: 65 us -> 63.1 us
    pallas_call x2, Pallas kernels: 42.9 us -> 40.9 us  [the longest x1 20.6 us: on_device(): pl.pallas_call(backward_kernel, out_shape=(jax.ShapeDtypeStruct((N_GA, 40...]
  transfers between devices with their start and end apart: 5 -> 5, of which waited for: 4 -> 4; matrix products, arithmetic and copies ran while one was open for 2% -> 2% of each run, Pallas kernels for 44% -> 43%
where the time goes in v4:
time: 134 us; the launch traced here: 133 us
  Pallas kernels  63.1 us (47%)
  blocking collectives  21.6 us (16%)
  waiting for transfers between devices  15.9 us (12%)
  between operations  14.1 us (11%)
  starting transfers between devices  9.08 us (7%)
  other arithmetic  4.79 us (4%)
  local copies, waits for them, and re-layouts  3.98 us (3%)
    pallas_call x1, Pallas kernels, on_device(): pl.pallas_call(backward_kernel, out_shape=(jax.ShapeDtypeStruct((N_GA, 40...  20.6 us
    pallas_call x1, Pallas kernels, on_device(): pl.pallas_call(forward_kernel, out_shape=(pltpu.VMEM((row_count, 128), f3...  20.3 us
    all_to_all x1, waiting for transfers between devices, on_device(): lax.all_to_all(sent, 'ga', split_axis=0, concat_axis=0, tiled=True)  11.4 us
    all_to_all x1, blocking collectives, on_device(): lax.all_to_all(shared, 'ga', split_axis=0, concat_axis=0, tiled=True)  11.4 us
    all_to_all x1, blocking collectives, on_device(): lax.all_to_all(gram, ('band', 'ga'), split_axis=0, concat_axis=0, tiled=T...  10.2 us
    pallas_call x1, Pallas kernels, on_device(): pl.pallas_call(prepare_kernel, out_shape=(jax.ShapeDtypeStruct((HALF * N,...  10.1 us
    pallas_call x1, Pallas kernels, on_device(): pl.pallas_call(gram_kernel, out_shape=jax.ShapeDtypeStruct((16, 2 * bands...  5.76 us
    all_to_all x1, starting transfers between devices, on_device(): lax.all_to_all(depth.reshape(N_GA, 40, COLS), 'ga', split_axis=0, concat_...  5.4 us
  transfers between devices with their start and end apart: 5, of which 4 were waited for; matrix products, arithmetic and copies ran while one was open for 2% of the time, Pallas kernels for 43%

profile of v4, /device:TPU:0, one launch (start us, length us, event | category | flops | bytes accessed | tf_op | source)
XLA Modules:
  0.0 132.5 jit_solution(12307242325864278719)
XLA Ops:
  7.2 1.2 fusion
  8.5 1.7 %collective-permute-done.1 = f32[2,80,640]{2,1,0:T(8,128)S(1)} collective-permute-done((f32[2,80,640]{2,1,0:T(8,128)S(1)}, f32[2,80,640]{2,1,0:T(8,128)S(1)}, u32[]{:S(2)}, u32[]{:S(2)}) %collective-permute-start.1) | collective-permute-done | bytes 409632 | tf_op jit(solution)/shard_map/ppermute | solution.py:456
  10.3 1.0 maximum_select_fusion
  11.3 2.9 %depth.1 = f32[320,640]{1,0:T(8,128)} custom-call(bf16[320,960]{1,0:T(8,128)(2,1)} %constant.121.clone.matrix, f32[320,640]{1,0:T(8,128)} %bitcast.32), custom_call_target="tpu_custom_call" | custom-call | tf_op jit(solution)/shard_map/depth/pallas_call | solution.py:462
  14.2 5.4 %all-to-all-start = ((f32[8,40,640]{2,1,0:T(8,128)}), f32[8,40,640]{2,1,0:T(8,128)S(1)}, u32[]{:S(2)}, u32[]{:S(2)}) async-start(f32[8,40,640]{2,1,0:T(8,128)} %bitcast.35), calls=%async_computation | async-start | bytes 1638400 | tf_op jit(solution)/shard_map/all_to_all | solution.py:470
  19.7 0.6 and_select_fusion
  20.3 10.1 %prepare.1 = (f32[12800,128]{1,0:T(8,128)}, f32[7680,128]{1,0:T(8,128)}) custom-call(s32[192]{0:T(256)} %get-tuple-element.24.box_plane, s32[192]{0:T(256)} %get-tuple-element.22.box_odd, f32[20,160,160]{2,1,0:T(8,128)} %potential.1, f32[192,128]{1,0:T(8,128)} %box_beta.1), custom_call_target="tpu_custom_call" | custom-call | bytes 14000000 | tf_op jit(solution)/shard_map/prepare/pallas_call | solution.py:479
  30.4 1.2 subtract_add_fusion.box_base
  31.7 0.7 fusion.3
  32.3 0.8 all-to-all-done.recv
  33.1 0.9 copy-done
  34.0 20.3 %planes_forward.1 = (f32[13440,128]{1,0:T(8,128)S(1)}, f32[8,8,256]{2,1,0:T(8,128)}) custom-call(s32[5120]{0:T(1024)} %get-tuple-element.28.site_row, s32[192]{0:T(256)} %subtract_add_fusion.box_base, f32[8,40,640]{2,1,0:T(8,128)} %copy-done, bf16[160,960]{1,0:T(8,128)(2,1)} %constant.122.clone.first_matrix, bf16[160,960]{1,0:T(8,128)(2,1)} %constant.123.clone.second_matrix, ...), custom_call_target="tpu_custom_call" | custom-call | tf_op jit(solution)/shard_map/planes_forward/pallas_call | solution.py:497
  54.3 11.4 %all_to_all.24.shared = f32[8,8,256]{2,1,0:T(8,128)} all-to-all(f32[8,8,256]{2,1,0:T(8,128)} %get-tuple-element.11), channel_id=1, replica_groups=mesh['band'=16,'ga'=8] {'ga'}, dimensions={0} | all-to-all | bytes 131072 | tf_op jit(solution)/shard_map/all_to_all | solution.py:526
  65.7 20.6 %planes_backward.1 = (f32[8,40,640]{2,1,0:T(8,128)}, f32[13440,128]{1,0:T(8,128)S(1)}) custom-call(s32[5120]{0:T(1024)} %get-tuple-element.29.site_row, s32[192]{0:T(256)} %subtract_add_fusion.box_base, f32[8,8,256]{2,1,0:T(8,128)} %all_to_all.24.shared, f32[1,1024]{1,0:T(1,128)} %bitcast.42, s32[1,192]{1,0:T(1,128)} %bitcast.44, ...), custom_call_target="tpu_custom_call", output_to_operand_aliasing={{1}: (8, {})} | custom-call | tf_op jit(solution)/shard_map/planes_backward/pallas_call | solution.py:527
  86.3 3.6 %all-to-all-start.2 = ((f32[8,40,640]{2,1,0:T(8,128)}), f32[8,40,640]{2,1,0:T(8,128)S(1)}, u32[]{:S(2)}, u32[]{:S(2)}) async-start(f32[8,40,640]{2,1,0:T(8,128)} %get-tuple-element.13), calls=%async_computation.2 | async-start | bytes 1638400 | tf_op jit(solution)/shard_map/all_to_all | solution.py:555
  90.0 0.6 reshape.133.plane_kinetic
  90.6 11.4 %all-to-all-done.2 = f32[8,40,640]{2,1,0:T(8,128)S(1)} async-done(((f32[8,40,640]{2,1,0:T(8,128)}), f32[8,40,640]{2,1,0:T(8,128)S(1)}, u32[]{:S(2)}, u32[]{:S(2)}) %all-to-all-start.2) | async-done | bytes 819232 | tf_op jit(solution)/shard_map/all_to_all | solution.py:555
  102.0 0.9 copy-done.1
  102.9 3.3 %finish.1 = (f32[320,640]{1,0:T(8,128)}, f32[160,640]{1,0:T(8,128)}) custom-call(s32[1]{0:T(128)} %bitcast.core, bf16[320,960]{1,0:T(8,128)(2,1)} %constant.126.clone.matrix, f32[320,640]{1,0:T(8,128)} %bitcast.34, f32[320,640]{1,0:T(8,128)} %bitcast.33, f32[1,640]{1,0:T(1,128)} %reshape.133.plane_kinetic), custom_call_target="tpu_custom_call" | custom-call | tf_op jit(solution)/shard_map/finish/pallas_call | solution.py:559
  106.2 2.0 %collective-permute-done.brought = f32[160,640]{1,0:T(8,128)S(1)} collective-permute-done((f32[160,640]{1,0:T(8,128)}, f32[160,640]{1,0:T(8,128)S(1)}, u32[]{:S(2)}, u32[]{:S(2)}) %collective-permute-start) | collective-permute-done | bytes 409632 | tf_op jit(solution)/shard_map/ppermute | solution.py:573
  108.2 0.8 copy-done.2
  108.9 5.8 %gram.1 = f32[16,32]{1,0:T(8,128)} custom-call(s32[1]{0:T(128)} %bitcast.core, f32[320,640]{1,0:T(8,128)} %get-tuple-element.14.result, f32[160,640]{1,0:T(8,128)} %copy-done.2, f32[8,2,160,640]{3,2,1,0:T(8,128)} %all-gather.2.cloned.1.call-done.basis_all), custom_call_target="tpu_custom_call" | custom-call | tf_op jit(solution)/shard_map/gram/pallas_call | solution.py:574
  114.7 10.2 %all_to_all.25 = f32[16,1,32]{2,1,0:T(1,128)S(1)} all-to-all(f32[16,1,32]{2,1,0:T(1,128)} %bitcast.40), channel_id=1, replica_groups={{0,1,2,3,4,5,6,7,8,9,10,11,12,13,14,15},{16,17,18,19,20,21,22,23,24,25,..., dimensions={0} | all-to-all | bytes 4096 | tf_op jit(solution)/shard_map/all_to_all | solution.py:589
  125.1 0.7 copy.29
  (17 shorter events, 0.5 us)
Async XLA Ops:
  7.2 12.4 %copy-start.3 = (s32[192,128]{1,0:T(8,128)S(1)}, s32[192,128]{1,0:T(8,128)}, u32[]{:S(2)}) copy-start(s32[192,128]{1,0:T(8,128)} %param.18) | copy-start | bytes 294916
  7.2 24.5 %copy-start.4 = (s32[5120]{0:T(1024)S(1)}, s32[5120]{0:T(1024)}, u32[]{:S(2)}) copy-start(s32[5120]{0:T(1024)} %param.16) | copy-start | bytes 61444
  7.2 101.0 %all-gather.2.cloned.1.call-start = ((), (), s32[]{:S(2)}) async-start(), calls=%async_computation.4 | async-start | bytes 7372800 | tf_op jit(solution)/shard_map/all_gather | solution.py:460
  8.4 1.8 %collective-permute-start.1 = (f32[2,80,640]{2,1,0:T(8,128)S(1)}, f32[2,80,640]{2,1,0:T(8,128)S(1)}, u32[]{:S(2)}, u32[]{:S(2)}) collective-permute-start(f32[2,80,640]{2,1,0:T(8,128)S(1)} %get-tuple-element.26), channel_id=1, source_target_pairs={{0,8},{8,0},{16,24},{24,16},{32,40},{40,32},{48,56},{56,48},{64,72... | collective-permute-start | bytes 1228808 | tf_op jit(solution)/shard_map/ppermute | solution.py:456
  14.2 18.9 %all-to-all-start = ((f32[8,40,640]{2,1,0:T(8,128)}), f32[8,40,640]{2,1,0:T(8,128)S(1)}, u32[]{:S(2)}, u32[]{:S(2)}) async-start(f32[8,40,640]{2,1,0:T(8,128)} %bitcast.35), calls=%async_computation | async-start | bytes 1638400 | tf_op jit(solution)/shard_map/all_to_all | solution.py:470
  33.1 0.9 copy-start
  86.3 15.6 %all-to-all-start.2 = ((f32[8,40,640]{2,1,0:T(8,128)}), f32[8,40,640]{2,1,0:T(8,128)S(1)}, u32[]{:S(2)}, u32[]{:S(2)}) async-start(f32[8,40,640]{2,1,0:T(8,128)} %get-tuple-element.13), calls=%async_computation.2 | async-start | bytes 1638400 | tf_op jit(solution)/shard_map/all_to_all | solution.py:555
  102.0 0.9 copy-start.1
  106.2 2.0 %collective-permute-start = (f32[160,640]{1,0:T(8,128)}, f32[160,640]{1,0:T(8,128)S(1)}, u32[]{:S(2)}, u32[]{:S(2)}) collective-permute-start(f32[160,640]{1,0:T(8,128)} %get-tuple-element.15), channel_id=1, source_target_pairs={{0,8},{8,0},{16,24},{24,16},{32,40},{40,32},{48,56},{56,48},{64,72... | collective-permute-start | bytes 1228808 | tf_op jit(solution)/shard_map/ppermute | solution.py:573
  108.1 0.8 copy-start.2
Sparse Core Ops, SparseCore 0:
  11.4 87.5 all-gather.1

commit v5 on v4

--- a/solution.py
+++ b/solution.py
@@ -19,8 +19,7 @@
 ATOMS = 1024
 GROUP = 40
 PITCH = 164
-LIMIT = 60 * 1024 * 1024
-KEPT = 8 * 1024 * 1024
+MIB = 1024 * 1024
 bf16 = jnp.bfloat16
 f32 = jnp.float32
 
@@ -453,20 +452,23 @@
     swap = [(i, i ^ 1) for i in range(bands)]
     kept = jnp.where(core == 0, halves[:, 0], halves[:, 1])
     given = jnp.where(core == 0, halves[:, 1], halves[:, 0])
+    trial = trial_bands.reshape(2 * N, COLS)
     taken = lax.ppermute(given, "band", swap)
-    block = jnp.where(core == 0, jnp.stack([kept, taken]), jnp.stack([taken, kept])).reshape(2, N, COLS)
-    chip_order = list(range(0, bands // 2, 2)) + list(range(bands // 2 - 1, 0, -2))
-    rings = [[2 * chip + k for chip in chip_order] for k in range(2)]
-    basis_all = lax.all_gather(block, "band", axis=0, axis_index_groups=rings)
-    trial = trial_bands.reshape(2 * N, COLS)
     depth = pl.pallas_call(
         depth_kernel,
         out_shape=jax.ShapeDtypeStruct((2 * N, COLS), f32),
         in_specs=[whole()] * 2,
         out_specs=whole(),
-        compiler_params=pltpu.CompilerParams(vmem_limit_bytes=LIMIT),
+        compiler_params=pltpu.CompilerParams(vmem_limit_bytes=60 * MIB),
+        cost_estimate=pl.CostEstimate(flops=2000000000, bytes_accessed=8000000, transcendentals=0),
         name="depth",
     )(jnp.asarray(forward_depth), trial)
+    taken, depth = lax.optimization_barrier((taken, depth))
+    block = jnp.where(core == 0, jnp.stack([kept, taken]), jnp.stack([taken, kept])).reshape(2, N, COLS)
+    depth, block = lax.optimization_barrier((depth, block))
+    chip_order = list(range(0, bands // 2, 2)) + list(range(bands // 2 - 1, 0, -2))
+    rings = [[2 * chip + k for chip in chip_order] for k in range(2)]
+    basis_all = lax.all_gather(block, "band", axis=0, axis_index_groups=rings)
     recv = lax.all_to_all(depth.reshape(N_GA, 40, COLS), "ga", split_axis=0, concat_axis=0, tiled=True)
 
     site_x = column_sites // N
@@ -489,7 +491,7 @@
             pltpu.VMEM((SLOTS * 40, 128), f32),
             pltpu.SemaphoreType.DMA((6,)),
         ],
-        compiler_params=pltpu.CompilerParams(vmem_limit_bytes=LIMIT),
+        compiler_params=pltpu.CompilerParams(vmem_limit_bytes=57 * MIB),
         cost_estimate=pl.CostEstimate(flops=0, bytes_accessed=14000000, transcendentals=0),
         name="prepare",
     )(corner_plane, corner_x % 2, potential, box_beta)
@@ -511,7 +513,7 @@
             pltpu.VMEM((SLOTS * 40, 128), f32),
             pltpu.SemaphoreType.DMA((2,)),
         ],
-        compiler_params=pltpu.CompilerParams(vmem_limit_bytes=LIMIT - KEPT),
+        compiler_params=pltpu.CompilerParams(vmem_limit_bytes=50 * MIB),
         name="planes_forward",
     )(
         site_y * N + site_x,
@@ -538,7 +540,7 @@
             pltpu.VMEM((SLOTS, 128), f32),
             pltpu.SemaphoreType.DMA((1,)),
         ],
-        compiler_params=pltpu.CompilerParams(vmem_limit_bytes=LIMIT - KEPT),
+        compiler_params=pltpu.CompilerParams(vmem_limit_bytes=44 * MIB),
         name="planes_backward",
     )(
         (site_y // 2) * N + site_x,
@@ -561,7 +563,7 @@
         out_shape=(jax.ShapeDtypeStruct((2 * N, COLS), f32), jax.ShapeDtypeStruct((N, COLS), f32)),
         in_specs=[whole(pltpu.SMEM)] + [whole()] * 4,
         out_specs=(whole(), whole()),
-        compiler_params=pltpu.CompilerParams(vmem_limit_bytes=LIMIT),
+        compiler_params=pltpu.CompilerParams(vmem_limit_bytes=57 * MIB),
         name="finish",
     )(
         core_number,
@@ -582,7 +584,7 @@
             pltpu.VMEM((2 * bands, 128), f32),
             pltpu.SemaphoreType.DMA((bands // 2,)),
         ],
-        compiler_params=pltpu.CompilerParams(vmem_limit_bytes=LIMIT),
+        compiler_params=pltpu.CompilerParams(vmem_limit_bytes=60 * MIB),
         name="gram",
     )(core_number, result, brought, basis_all)
     chip_group = [[(2 * chip + k) * N_GA + g for k in range(2) for g in range(N_GA)] for chip in range(bands // 2)]

time: 134 us -> 133 us (level)
    ppermute x1, waiting for transfers between devices: 1.73 us -> 0.01 us  [on_device(): taken = lax.ppermute(given, 'band', swap)]
    all_to_all x1, waiting for transfers between devices: 11.4 us -> 12.8 us  [on_device(): lax.all_to_all(sent, 'ga', split_axis=0, concat_axis=0, tiled=True)]
    unnamed x11 -> x21, local copies, waits for them, and re-layouts: 3.21 us -> 3.22 us
  transfers between devices with their start and end apart: 5 -> 5, of which waited for: 4 -> 3; matrix products, arithmetic and copies ran while one was open for 2% -> 3% of each run, Pallas kernels for 43% -> 43%
where the time goes in v5:
time: 133 us; the launch traced here: 131 us
  Pallas kernels  62.9 us (47%)
  blocking collectives  20.4 us (15%)
  waiting for transfers between devices  15.9 us (12%)
  between operations  14.2 us (11%)
  starting transfers between devices  9.1 us (7%)
  other arithmetic  4.84 us (4%)
  local copies, waits for them, and re-layouts  4.01 us (3%)
    pallas_call x1, Pallas kernels, on_device(): pl.pallas_call(backward_kernel, out_shape=(jax.ShapeDtypeStruct((N_GA, 40...  20.4 us
    pallas_call x1, Pallas kernels, on_device(): pl.pallas_call(forward_kernel, out_shape=(pltpu.VMEM((row_count, 128), f3...  20.3 us
    all_to_all x1, waiting for transfers between devices, on_device(): lax.all_to_all(sent, 'ga', split_axis=0, concat_axis=0, tiled=True)  12.8 us
    all_to_all x1, blocking collectives, on_device(): lax.all_to_all(shared, 'ga', split_axis=0, concat_axis=0, tiled=True)  10.9 us
    pallas_call x1, Pallas kernels, on_device(): pl.pallas_call(prepare_kernel, out_shape=(jax.ShapeDtypeStruct((HALF * N,...  10.1 us
    all_to_all x1, blocking collectives, on_device(): lax.all_to_all(gram, ('band', 'ga'), split_axis=0, concat_axis=0, tiled=T...  9.51 us
    pallas_call x1, Pallas kernels, on_device(): pl.pallas_call(gram_kernel, out_shape=jax.ShapeDtypeStruct((16, 2 * bands...  5.76 us
    all_to_all x1, starting transfers between devices, on_device(): lax.all_to_all(depth.reshape(N_GA, 40, COLS), 'ga', split_axis=0, concat_...  5.41 us
  transfers between devices with their start and end apart: 5, of which 3 were waited for; matrix products, arithmetic and copies ran while one was open for 3% of the time, Pallas kernels for 43%

profile of v5, /device:TPU:0, one launch (start us, length us, event | category | flops | bytes accessed | tf_op | source)
XLA Modules:
  0.0 131.3 jit_solution(2806167551420434666)
XLA Ops:
  7.2 1.2 fusion
  8.6 2.9 %depth.1 = f32[320,640]{1,0:T(8,128)} custom-call(bf16[320,960]{1,0:T(8,128)(2,1)} %constant.121.clone.matrix, f32[320,640]{1,0:T(8,128)} %bitcast.41), custom_call_target="tpu_custom_call" | custom-call | flops 2000000000 | bytes 8000000 | tf_op jit(solution)/shard_map/depth/pallas_call | solution.py:457
  11.5 1.0 maximum_select_fusion
  12.5 5.4 %all-to-all-start = ((f32[8,40,640]{2,1,0:T(8,128)}), f32[8,40,640]{2,1,0:T(8,128)S(1)}, u32[]{:S(2)}, u32[]{:S(2)}) async-start(f32[8,40,640]{2,1,0:T(8,128)} %bitcast.43), calls=%async_computation | async-start | bytes 1638400 | tf_op jit(solution)/shard_map/all_to_all | solution.py:472
  17.9 0.1 slice_reduce_fusion
  18.0 0.6 and_select_fusion
  18.6 10.1 %prepare.1 = (f32[12800,128]{1,0:T(8,128)}, f32[7680,128]{1,0:T(8,128)}) custom-call(s32[192]{0:T(256)} %get-tuple-element.32.box_plane, s32[192]{0:T(256)} %get-tuple-element.30.box_odd, f32[20,160,160]{2,1,0:T(8,128)} %potential.1, f32[192,128]{1,0:T(8,128)} %box_beta.1), custom_call_target="tpu_custom_call" | custom-call | bytes 14000000 | tf_op jit(solution)/shard_map/prepare/pallas_call | solution.py:481
  28.8 1.3 subtract_add_fusion.box_base
  30.1 0.6 fusion.3
  30.7 1.1 all-to-all-done.recv
  31.9 0.9 copy-done.5
  32.8 20.3 %planes_forward.1 = (f32[13440,128]{1,0:T(8,128)S(1)}, f32[8,8,256]{2,1,0:T(8,128)}) custom-call(s32[5120]{0:T(1024)} %get-tuple-element.36.site_row, s32[192]{0:T(256)} %subtract_add_fusion.box_base, f32[8,40,640]{2,1,0:T(8,128)} %copy-done.5, bf16[160,960]{1,0:T(8,128)(2,1)} %constant.122.clone.first_matrix, ...), custom_call_target="tpu_custom_call" | custom-call | tf_op jit(solution)/shard_map/planes_forward/pallas_call | solution.py:499
  53.1 10.9 %all_to_all.24.shared = f32[8,8,256]{2,1,0:T(8,128)S(1)} all-to-all(f32[8,8,256]{2,1,0:T(8,128)} %get-tuple-element.18), channel_id=1, replica_groups=mesh['band'=16,'ga'=8] {'ga'}, dimensions={0} | all-to-all | bytes 131072 | tf_op jit(solution)/shard_map/all_to_all | solution.py:528
  64.0 20.4 %planes_backward.1 = (f32[8,40,640]{2,1,0:T(8,128)}, f32[13440,128]{1,0:T(8,128)S(1)}) custom-call(s32[5120]{0:T(1024)S(1)} %get-tuple-element.37.site_row, s32[192]{0:T(256)S(1)} %copy-done.2, f32[8,8,256]{2,1,0:T(8,128)S(1)} %all_to_all.24.shared, f32[1,1024]{1,0:T(1,128)S(1)} %bitcast.33, s32[1,192]{1,0:T(1,128)S(1)} %bitcast.35, ...), custom_call_target="tpu_custom_call", output_to_operand_aliasing={{1}: (8, {})} | custom-call | tf_op jit(solution)/shard_map/planes_backward/pallas_call | solution.py:529
  84.5 3.6 %all-to-all-start.2 = ((f32[8,40,640]{2,1,0:T(8,128)}), f32[8,40,640]{2,1,0:T(8,128)S(1)}, u32[]{:S(2)}, u32[]{:S(2)}) async-start(f32[8,40,640]{2,1,0:T(8,128)} %get-tuple-element.20), calls=%async_computation.2 | async-start | bytes 1638400 | tf_op jit(solution)/shard_map/all_to_all | solution.py:557
  88.1 0.6 reshape.79.plane_kinetic
  88.7 12.8 %all-to-all-done.2 = f32[8,40,640]{2,1,0:T(8,128)S(1)} async-done(((f32[8,40,640]{2,1,0:T(8,128)}), f32[8,40,640]{2,1,0:T(8,128)S(1)}, u32[]{:S(2)}, u32[]{:S(2)}) %all-to-all-start.2) | async-done | bytes 819232 | tf_op jit(solution)/shard_map/all_to_all | solution.py:557
  101.5 0.9 copy-done.6
  102.4 3.3 %finish.1 = (f32[320,640]{1,0:T(8,128)}, f32[160,640]{1,0:T(8,128)}) custom-call(s32[1]{0:T(128)} %bitcast.core, bf16[320,960]{1,0:T(8,128)(2,1)} %constant.126.clone.matrix, f32[320,640]{1,0:T(8,128)} %bitcast.37, f32[320,640]{1,0:T(8,128)} %bitcast.42, f32[1,640]{1,0:T(1,128)} %reshape.79.plane_kinetic), custom_call_target="tpu_custom_call" | custom-call | tf_op jit(solution)/shard_map/finish/pallas_call | solution.py:561
  105.7 2.0 %collective-permute-done.1.brought = f32[160,640]{1,0:T(8,128)S(1)} collective-permute-done((f32[160,640]{1,0:T(8,128)}, f32[160,640]{1,0:T(8,128)S(1)}, u32[]{:S(2)}, u32[]{:S(2)}) %collective-permute-start.1) | collective-permute-done | bytes 409632 | tf_op jit(solution)/shard_map/ppermute | solution.py:575
  107.7 0.8 copy-done.7
  108.4 5.8 %gram.1 = f32[16,32]{1,0:T(8,128)} custom-call(s32[1]{0:T(128)} %bitcast.core, f32[320,640]{1,0:T(8,128)} %get-tuple-element.21.result, f32[160,640]{1,0:T(8,128)} %copy-done.7, f32[8,2,160,640]{3,2,1,0:T(8,128)} %bitcast.36), custom_call_target="tpu_custom_call" | custom-call | tf_op jit(solution)/shard_map/gram/pallas_call | solution.py:576
  114.2 9.5 %all_to_all.25 = f32[16,1,32]{2,1,0:T(1,128)S(1)} all-to-all(f32[16,1,32]{2,1,0:T(1,128)} %bitcast.45), channel_id=1, replica_groups={{0,1,2,3,4,5,6,7,8,9,10,11,12,13,14,15},{16,17,18,19,20,21,22,23,24,25,..., dimensions={0} | all-to-all | bytes 4096 | tf_op jit(solution)/shard_map/all_to_all | solution.py:591
  123.8 0.7 copy.25
  (27 shorter events, 0.4 us)
Async XLA Ops:
  7.2 100.5 %all-gather.3.cloned.1.call-start = ((), (), s32[]{:S(2)}) async-start(), calls=%async_computation.4 | async-start | bytes 7372800 | tf_op jit(solution)/shard_map/all_gather | solution.py:471
  7.2 10.7 %copy-start.8 = (s32[192,128]{1,0:T(8,128)S(1)}, s32[192,128]{1,0:T(8,128)}, u32[]{:S(2)}) copy-start(s32[192,128]{1,0:T(8,128)} %param.18) | copy-start | bytes 294916
  8.5 3.0 %collective-permute-start = (f32[2,80,640]{2,1,0:T(8,128)S(1)}, f32[2,80,640]{2,1,0:T(8,128)S(1)}, u32[]{:S(2)}, u32[]{:S(2)}) collective-permute-start(f32[2,80,640]{2,1,0:T(8,128)S(1)} %get-tuple-element.34), channel_id=1, source_target_pairs={{0,8},{8,0},{16,24},{24,16},{32,40},{40,32},{48,56},{56,48},{64,72... | collective-permute-start | bytes 1228808 | tf_op jit(solution)/shard_map/ppermute | solution.py:456
  8.6 21.5 %copy-start.9 = (s32[5120]{0:T(1024)S(1)}, s32[5120]{0:T(1024)}, u32[]{:S(2)}) copy-start(s32[5120]{0:T(1024)} %param.16) | copy-start | bytes 61444
  12.5 19.4 %all-to-all-start = ((f32[8,40,640]{2,1,0:T(8,128)}), f32[8,40,640]{2,1,0:T(8,128)S(1)}, u32[]{:S(2)}, u32[]{:S(2)}) async-start(f32[8,40,640]{2,1,0:T(8,128)} %bitcast.43), calls=%async_computation | async-start | bytes 1638400 | tf_op jit(solution)/shard_map/all_to_all | solution.py:472
  28.7 35.2 %copy-start = (bf16[160,960]{1,0:T(8,128)(2,1)S(1)}, bf16[160,960]{1,0:T(8,128)(2,1)}, u32[]{:S(2)}) copy-start(bf16[160,960]{1,0:T(8,128)(2,1)} %constant.124.clone.first_matrix) | copy-start | bytes 921604
  28.8 35.2 %copy-start.1 = (bf16[160,960]{1,0:T(8,128)(2,1)S(1)}, bf16[160,960]{1,0:T(8,128)(2,1)}, u32[]{:S(2)}) copy-start(bf16[160,960]{1,0:T(8,128)(2,1)} %constant.125.clone.second_matrix) | copy-start | bytes 921604
  28.8 35.2 %copy-start.3 = (f32[1024]{0:T(1024)S(1)}, f32[1024]{0:T(1024)}, u32[]{:S(2)}) copy-start(f32[1024]{0:T(1024)} %param.21) | copy-start | bytes 12292
  28.8 35.2 %copy-start.4 = (s32[192]{0:T(256)S(1)}, s32[192]{0:T(256)}, u32[]{:S(2)}) copy-start(s32[192]{0:T(256)} %param.19) | copy-start | bytes 2308
  30.1 33.9 %copy-start.2 = (s32[192]{0:T(256)S(1)}, s32[192]{0:T(256)}, u32[]{:S(2)}) copy-start(s32[192]{0:T(256)} %subtract_add_fusion.box_base) | copy-start | bytes 2308
  31.9 0.9 copy-start.5
  84.5 17.0 %all-to-all-start.2 = ((f32[8,40,640]{2,1,0:T(8,128)}), f32[8,40,640]{2,1,0:T(8,128)S(1)}, u32[]{:S(2)}, u32[]{:S(2)}) async-start(f32[8,40,640]{2,1,0:T(8,128)} %get-tuple-element.20), calls=%async_computation.2 | async-start | bytes 1638400 | tf_op jit(solution)/shard_map/all_to_all | solution.py:557
  101.5 0.9 copy-start.6
  105.7 2.0 %collective-permute-start.1 = (f32[160,640]{1,0:T(8,128)}, f32[160,640]{1,0:T(8,128)S(1)}, u32[]{:S(2)}, u32[]{:S(2)}) collective-permute-start(f32[160,640]{1,0:T(8,128)} %get-tuple-element.22), channel_id=1, source_target_pairs={{0,8},{8,0},{16,24},{24,16},{32,40},{40,32},{48,56},{56,48},{64,72... | collective-permute-start | bytes 1228808 | tf_op jit(solution)/shard_map/ppermute | solution.py:575
  107.6 0.8 copy-start.7
Sparse Core Ops, SparseCore 0:
  12.6 90.9 all-gather.2

commit v6 on v5

--- a/solution.py
+++ b/solution.py
@@ -563,7 +563,7 @@
         out_shape=(jax.ShapeDtypeStruct((2 * N, COLS), f32), jax.ShapeDtypeStruct((N, COLS), f32)),
         in_specs=[whole(pltpu.SMEM)] + [whole()] * 4,
         out_specs=(whole(), whole()),
-        compiler_params=pltpu.CompilerParams(vmem_limit_bytes=57 * MIB),
+        compiler_params=pltpu.CompilerParams(vmem_limit_bytes=24 * MIB),
         name="finish",
     )(
         core_number,

time: 133 us -> 130 us (0.977)
  Pallas kernels: 62.9 us -> 61.2 us
  local copies, waits for them, and re-layouts: 4.01 us -> 2.56 us
    pallas_call x1, Pallas kernels: 3.32 us -> 1.61 us  [on_device(): pl.pallas_call(finish_kernel, out_shape=(jax.ShapeDtypeStruct((2 * N, COL...]
    unnamed x21 -> x23, local copies, waits for them, and re-layouts: 3.22 us -> 2.36 us
  transfers between devices with their start and end apart: 5 -> 5, of which waited for: 3 -> 3; matrix products, arithmetic and copies ran while one was open for 3% -> 2% of each run, Pallas kernels for 43% -> 43%
where the time goes in v6:
time: 130 us; the launch traced here: 129 us
  Pallas kernels  61.2 us (47%)
  blocking collectives  20.4 us (16%)
  waiting for transfers between devices  16.2 us (12%)
  between operations  14.2 us (11%)
  starting transfers between devices  9.1 us (7%)
  other arithmetic  4.83 us (4%)
  local copies, waits for them, and re-layouts  2.56 us (2%)
    pallas_call x1, Pallas kernels, on_device(): pl.pallas_call(backward_kernel, out_shape=(jax.ShapeDtypeStruct((N_GA, 40...  20.4 us
    pallas_call x1, Pallas kernels, on_device(): pl.pallas_call(forward_kernel, out_shape=(pltpu.VMEM((row_count, 128), f3...  20.3 us
    all_to_all x1, waiting for transfers between devices, on_device(): lax.all_to_all(sent, 'ga', split_axis=0, concat_axis=0, tiled=True)  13.3 us
    all_to_all x1, blocking collectives, on_device(): lax.all_to_all(shared, 'ga', split_axis=0, concat_axis=0, tiled=True)  10.9 us
    pallas_call x1, Pallas kernels, on_device(): pl.pallas_call(prepare_kernel, out_shape=(jax.ShapeDtypeStruct((HALF * N,...  10.2 us
    all_to_all x1, blocking collectives, on_device(): lax.all_to_all(gram, ('band', 'ga'), split_axis=0, concat_axis=0, tiled=T...  9.52 us
    pallas_call x1, Pallas kernels, on_device(): pl.pallas_call(gram_kernel, out_shape=jax.ShapeDtypeStruct((16, 2 * bands...  5.77 us
    all_to_all x1, starting transfers between devices, on_device(): lax.all_to_all(depth.reshape(N_GA, 40, COLS), 'ga', split_axis=0, concat_...  5.41 us
  transfers between devices with their start and end apart: 5, of which 3 were waited for; matrix products, arithmetic and copies ran while one was open for 2% of the time, Pallas kernels for 43%

profile of v6, /device:TPU:0, one launch (start us, length us, event | category | flops | bytes accessed | tf_op | source)
XLA Modules:
  0.0 128.5 jit_solution(10471284548428494159)
XLA Ops:
  7.2 1.2 fusion
  8.5 0.1 collective-permute-start
  8.6 2.9 %depth.1 = f32[320,640]{1,0:T(8,128)} custom-call(bf16[320,960]{1,0:T(8,128)(2,1)} %constant.121.clone.matrix, f32[320,640]{1,0:T(8,128)} %bitcast.34), custom_call_target="tpu_custom_call" | custom-call | flops 2000000000 | bytes 8000000 | tf_op jit(solution)/shard_map/depth/pallas_call | solution.py:457
  11.5 0.9 maximum_select_fusion
  12.5 5.4 %all-to-all-start = ((f32[8,40,640]{2,1,0:T(8,128)}), f32[8,40,640]{2,1,0:T(8,128)S(1)}, u32[]{:S(2)}, u32[]{:S(2)}) async-start(f32[8,40,640]{2,1,0:T(8,128)} %bitcast.43), calls=%async_computation | async-start | bytes 1638400 | tf_op jit(solution)/shard_map/all_to_all | solution.py:472
  17.9 0.1 slice_reduce_fusion
  18.0 0.6 and_select_fusion
  18.6 10.2 %prepare.1 = (f32[12800,128]{1,0:T(8,128)}, f32[7680,128]{1,0:T(8,128)}) custom-call(s32[192]{0:T(256)} %get-tuple-element.32.box_plane, s32[192]{0:T(256)} %get-tuple-element.30.box_odd, f32[20,160,160]{2,1,0:T(8,128)} %potential.1, f32[192,128]{1,0:T(8,128)} %box_beta.1), custom_call_target="tpu_custom_call" | custom-call | bytes 14000000 | tf_op jit(solution)/shard_map/prepare/pallas_call | solution.py:481
  28.8 1.3 %subtract_add_fusion.box_base = s32[192]{0:T(256)} fusion(s32[192]{0:T(256)S(1)} %get-tuple-element.31, s32[192]{0:T(256)S(1)} %slice_reduce_fusion, s32[192]{0:T(256)} %get-tuple-element.32.box_plane), kind=kLoop, calls=%fused_computation.43 | loop fusion | flops 4032 | bytes 3072 | tf_op jit(solution)/shard_map/add | solution.py:480
  30.1 0.6 fusion.3
  30.7 1.1 all-to-all-done.recv
  31.9 0.9 copy-done.7
  32.8 20.3 %planes_forward.1 = (f32[13440,128]{1,0:T(8,128)S(1)}, f32[8,8,256]{2,1,0:T(8,128)}) custom-call(s32[5120]{0:T(1024)} %get-tuple-element.36.site_row, s32[192]{0:T(256)} %subtract_add_fusion.box_base, f32[8,40,640]{2,1,0:T(8,128)} %copy-done.7, bf16[160,960]{1,0:T(8,128)(2,1)} %constant.122.clone.first_matrix, ...), custom_call_target="tpu_custom_call" | custom-call | tf_op jit(solution)/shard_map/planes_forward/pallas_call | solution.py:499
  53.0 10.9 %all_to_all.24.shared = f32[8,8,256]{2,1,0:T(8,128)S(1)} all-to-all(f32[8,8,256]{2,1,0:T(8,128)} %get-tuple-element.18), channel_id=1, replica_groups=mesh['band'=16,'ga'=8] {'ga'}, dimensions={0} | all-to-all | bytes 131072 | tf_op jit(solution)/shard_map/all_to_all | solution.py:528
  64.0 20.4 %planes_backward.1 = (f32[8,40,640]{2,1,0:T(8,128)}, f32[13440,128]{1,0:T(8,128)S(1)}) custom-call(s32[5120]{0:T(1024)S(1)} %get-tuple-element.37.site_row, s32[192]{0:T(256)S(1)} %copy-done.4, f32[8,8,256]{2,1,0:T(8,128)S(1)} %all_to_all.24.shared, f32[1,1024]{1,0:T(1,128)S(1)} %bitcast.36, s32[1,192]{1,0:T(1,128)S(1)} %bitcast.38, ...), custom_call_target="tpu_custom_call", output_to_operand_aliasing={{1}: (8, {})} | custom-call | tf_op jit(solution)/shard_map/planes_backward/pallas_call | solution.py:529
  84.5 3.6 %all-to-all-start.2 = ((f32[8,40,640]{2,1,0:T(8,128)}), f32[8,40,640]{2,1,0:T(8,128)S(1)}, u32[]{:S(2)}, u32[]{:S(2)}) async-start(f32[8,40,640]{2,1,0:T(8,128)} %get-tuple-element.20), calls=%async_computation.2 | async-start | bytes 1638400 | tf_op jit(solution)/shard_map/all_to_all | solution.py:557
  88.1 0.1 fusion.9
  88.2 13.3 %all-to-all-done.2 = f32[8,40,640]{2,1,0:T(8,128)S(1)} async-done(((f32[8,40,640]{2,1,0:T(8,128)}), f32[8,40,640]{2,1,0:T(8,128)S(1)}, u32[]{:S(2)}, u32[]{:S(2)}) %all-to-all-start.2) | async-done | bytes 819232 | tf_op jit(solution)/shard_map/all_to_all | solution.py:557
  101.5 1.6 %finish.1 = (f32[320,640]{1,0:T(8,128)}, f32[160,640]{1,0:T(8,128)S(1)}) custom-call(s32[1]{0:T(128)} %bitcast.core, bf16[320,960]{1,0:T(8,128)(2,1)S(1)} %copy-done.1, f32[320,640]{1,0:T(8,128)S(1)} %bitcast.33, f32[320,640]{1,0:T(8,128)S(1)} %bitcast.35, f32[1,640]{1,0:T(1,128)S(1)} %reshape.79.plane_kinetic), custom_call_target="tpu_custom_call" | custom-call | tf_op jit(solution)/shard_map/finish/pallas_call | solution.py:561
  103.1 1.7 %collective-permute-done.1.brought = f32[160,640]{1,0:T(8,128)S(1)} collective-permute-done((f32[160,640]{1,0:T(8,128)S(1)}, f32[160,640]{1,0:T(8,128)S(1)}, u32[]{:S(2)}, u32[]{:S(2)}) %collective-permute-start.1) | collective-permute-done | bytes 409632 | tf_op jit(solution)/shard_map/ppermute | solution.py:575
  104.8 0.8 copy-done.8
  105.6 5.8 %gram.1 = f32[16,32]{1,0:T(8,128)} custom-call(s32[1]{0:T(128)} %bitcast.core, f32[320,640]{1,0:T(8,128)} %get-tuple-element.21.result, f32[160,640]{1,0:T(8,128)} %copy-done.8, f32[8,2,160,640]{3,2,1,0:T(8,128)} %bitcast.39), custom_call_target="tpu_custom_call" | custom-call | tf_op jit(solution)/shard_map/gram/pallas_call | solution.py:576
  111.4 9.5 %all_to_all.25 = f32[16,1,32]{2,1,0:T(1,128)S(1)} all-to-all(f32[16,1,32]{2,1,0:T(1,128)} %bitcast.45), channel_id=1, replica_groups={{0,1,2,3,4,5,6,7,8,9,10,11,12,13,14,15},{16,17,18,19,20,21,22,23,24,25,..., dimensions={0} | all-to-all | bytes 4096 | tf_op jit(solution)/shard_map/all_to_all | solution.py:591
  121.0 0.7 copy.25
  (29 shorter events, 0.2 us)
Async XLA Ops:
  7.2 97.7 %all-gather.3.cloned.1.call-start = ((), (), s32[]{:S(2)}) async-start(), calls=%async_computation.4 | async-start | bytes 7372800 | tf_op jit(solution)/shard_map/all_gather | solution.py:471
  7.2 10.7 %copy-start.9 = (s32[192,128]{1,0:T(8,128)S(1)}, s32[192,128]{1,0:T(8,128)}, u32[]{:S(2)}) copy-start(s32[192,128]{1,0:T(8,128)} %param.18) | copy-start | bytes 294916
  8.5 3.0 %collective-permute-start = (f32[2,80,640]{2,1,0:T(8,128)S(1)}, f32[2,80,640]{2,1,0:T(8,128)S(1)}, u32[]{:S(2)}, u32[]{:S(2)}) collective-permute-start(f32[2,80,640]{2,1,0:T(8,128)S(1)} %get-tuple-element.34), channel_id=1, source_target_pairs={{0,8},{8,0},{16,24},{24,16},{32,40},{40,32},{48,56},{56,48},{64,72... | collective-permute-start | bytes 1228808 | tf_op jit(solution)/shard_map/ppermute | solution.py:456
  8.6 21.6 %copy-start.10 = (s32[5120]{0:T(1024)S(1)}, s32[5120]{0:T(1024)}, u32[]{:S(2)}) copy-start(s32[5120]{0:T(1024)} %param.16) | copy-start | bytes 61444
  12.5 19.4 %all-to-all-start = ((f32[8,40,640]{2,1,0:T(8,128)}), f32[8,40,640]{2,1,0:T(8,128)S(1)}, u32[]{:S(2)}, u32[]{:S(2)}) async-start(f32[8,40,640]{2,1,0:T(8,128)} %bitcast.43), calls=%async_computation | async-start | bytes 1638400 | tf_op jit(solution)/shard_map/all_to_all | solution.py:472
  28.8 35.2 %copy-start.2 = (bf16[160,960]{1,0:T(8,128)(2,1)S(1)}, bf16[160,960]{1,0:T(8,128)(2,1)}, u32[]{:S(2)}) copy-start(bf16[160,960]{1,0:T(8,128)(2,1)} %constant.124.clone.first_matrix) | copy-start | bytes 921604
  28.8 35.2 %copy-start.3 = (bf16[160,960]{1,0:T(8,128)(2,1)S(1)}, bf16[160,960]{1,0:T(8,128)(2,1)}, u32[]{:S(2)}) copy-start(bf16[160,960]{1,0:T(8,128)(2,1)} %constant.125.clone.second_matrix) | copy-start | bytes 921604
  28.8 35.2 %copy-start.5 = (f32[1024]{0:T(1024)S(1)}, f32[1024]{0:T(1024)}, u32[]{:S(2)}) copy-start(f32[1024]{0:T(1024)} %param.21) | copy-start | bytes 12292
  28.8 35.2 %copy-start.6 = (s32[192]{0:T(256)S(1)}, s32[192]{0:T(256)}, u32[]{:S(2)}) copy-start(s32[192]{0:T(256)} %param.19) | copy-start | bytes 2308
  30.1 33.9 %copy-start.4 = (s32[192]{0:T(256)S(1)}, s32[192]{0:T(256)}, u32[]{:S(2)}) copy-start(s32[192]{0:T(256)} %subtract_add_fusion.box_base) | copy-start | bytes 2308
  31.9 0.9 copy-start.7
  64.0 37.5 %copy-start = (f32[1,2,160,640]{3,2,1,0:T(8,128)S(1)}, f32[1,2,160,640]{3,2,1,0:T(8,128)}, u32[]{:S(2)}) copy-start(f32[1,2,160,640]{3,2,1,0:T(8,128)} %param.14) | copy-start | bytes 2457604
  64.0 37.5 %copy-start.1 = (bf16[320,960]{1,0:T(8,128)(2,1)S(1)}, bf16[320,960]{1,0:T(8,128)(2,1)}, u32[]{:S(2)}) copy-start(bf16[320,960]{1,0:T(8,128)(2,1)} %constant.126.clone.matrix) | copy-start | bytes 1843204
  84.5 17.0 %all-to-all-start.2 = ((f32[8,40,640]{2,1,0:T(8,128)}), f32[8,40,640]{2,1,0:T(8,128)S(1)}, u32[]{:S(2)}, u32[]{:S(2)}) async-start(f32[8,40,640]{2,1,0:T(8,128)} %get-tuple-element.20), calls=%async_computation.2 | async-start | bytes 1638400 | tf_op jit(solution)/shard_map/all_to_all | solution.py:557
  103.1 1.7 %collective-permute-start.1 = (f32[160,640]{1,0:T(8,128)S(1)}, f32[160,640]{1,0:T(8,128)S(1)}, u32[]{:S(2)}, u32[]{:S(2)}) collective-permute-start(f32[160,640]{1,0:T(8,128)S(1)} %get-tuple-element.22), channel_id=1, source_target_pairs={{0,8},{8,0},{16,24},{24,16},{32,40},{40,32},{48,56},{56,48},{64,72... | collective-permute-start | bytes 1228808 | tf_op jit(solution)/shard_map/ppermute | solution.py:575
  104.8 0.8 copy-start.8
Sparse Core Ops, SparseCore 0:
  12.6 90.9 all-gather.2

commit v7 on v6

--- a/solution.py
+++ b/solution.py
@@ -374,8 +374,8 @@
     beta_copy.wait()
 
     def add_boxes(t, carry):
-        for k in range(2):
-            s = t * 2 + k
+        for k in range(4):
+            s = t * 4 + k
             weight = weights[pl.ds(s, 1), :]
             places = box_places(box_base, s)
             olds = [applied[place, :] for place in places]
@@ -383,7 +383,7 @@
                 applied[places[i], :] = olds[i] + beta[pl.ds(pl.multiple_of(s * 40 + i * 8, 8), 8), :] * weight
         return carry
 
-    lax.fori_loop(0, SLOTS // 2, add_boxes, 0)
+    lax.fori_loop(0, SLOTS // 4, add_boxes, 0)
 
     def along_y(t, carry):
         blocks = []
@@ -491,7 +491,7 @@
             pltpu.VMEM((SLOTS * 40, 128), f32),
             pltpu.SemaphoreType.DMA((6,)),
         ],
-        compiler_params=pltpu.CompilerParams(vmem_limit_bytes=57 * MIB),
+        compiler_params=pltpu.CompilerParams(vmem_limit_bytes=24 * MIB),
         cost_estimate=pl.CostEstimate(flops=0, bytes_accessed=14000000, transcendentals=0),
         name="prepare",
     )(corner_plane, corner_x % 2, potential, box_beta)

time: 130 us -> 132 us (1.015)
  local copies, waits for them, and re-layouts: 2.56 us -> 6.29 us
  waiting for transfers between devices: 16.2 us -> 14 us
  Pallas kernels: 61.2 us -> 59.8 us
    unnamed x23 -> x29, local copies, waits for them, and re-layouts: 2.36 us -> 6.09 us
  transfers between devices with their start and end apart: 5 -> 5, of which waited for: 3 -> 2; matrix products, arithmetic and copies ran while one was open for 2% -> 1% of each run, Pallas kernels for 43% -> 41%
where the time goes in v7:
time: 132 us; the launch traced here: 130 us
  Pallas kernels  59.8 us (45%)
  blocking collectives  21.6 us (16%)
  between operations  14.2 us (11%)
  waiting for transfers between devices  14 us (11%)
  starting transfers between devices  9.01 us (7%)
  local copies, waits for them, and re-layouts  6.29 us (5%)
  other arithmetic  5.56 us (4%)
    pallas_call x1, Pallas kernels, on_device(): pl.pallas_call(forward_kernel, out_shape=(pltpu.VMEM((row_count, 128), f3...  20.3 us
    pallas_call x1, Pallas kernels, on_device(): pl.pallas_call(backward_kernel, out_shape=(jax.ShapeDtypeStruct((N_GA, 40...  20.1 us
    all_to_all x1, waiting for transfers between devices, on_device(): lax.all_to_all(sent, 'ga', split_axis=0, concat_axis=0, tiled=True)  12.2 us
    all_to_all x1, blocking collectives, on_device(): lax.all_to_all(shared, 'ga', split_axis=0, concat_axis=0, tiled=True)  12.1 us
    all_to_all x1, blocking collectives, on_device(): lax.all_to_all(gram, ('band', 'ga'), split_axis=0, concat_axis=0, tiled=T...  9.52 us
    pallas_call x1, Pallas kernels, on_device(): pl.pallas_call(prepare_kernel, out_shape=(jax.ShapeDtypeStruct((HALF * N,...  9.19 us
    unnamed x29, local copies, waits for them, and re-layouts  6.09 us
    pallas_call x1, Pallas kernels, on_device(): pl.pallas_call(gram_kernel, out_shape=jax.ShapeDtypeStruct((16, 2 * bands...  5.76 us
  transfers between devices with their start and end apart: 5, of which 2 were waited for; matrix products, arithmetic and copies ran while one was open for 1% of the time, Pallas kernels for 41%

profile of v7, /device:TPU:0, one launch (start us, length us, event | category | flops | bytes accessed | tf_op | source)
XLA Modules:
  0.0 130.5 jit_solution(15023215001152709853)
XLA Ops:
  7.2 0.0 all-gather.3.cloned.1.call-start
  7.3 2.1 %fusion = (f32[2,1,80,640]{3,2,0,1:T(8,128)S(1)}, f32[2,80,640]{2,1,0:T(8,128)}) fusion(f32[2,2,80,640]{3,2,1,0:T(8,128)} %bitcast.42, pred[]{:T(512)S(6)} %eq.9), kind=kLoop, calls=%fused_computation.4 | loop fusion | flops 204800 | bytes 1638401 | tf_op jit(solution)/shard_map/jit(_where)/select_n | solution.py:453
  9.3 2.9 %depth.1 = f32[320,640]{1,0:T(8,128)} custom-call(bf16[320,960]{1,0:T(8,128)(2,1)} %constant.121.clone.matrix, f32[320,640]{1,0:T(8,128)} %bitcast.34), custom_call_target="tpu_custom_call" | custom-call | flops 2000000000 | bytes 8000000 | tf_op jit(solution)/shard_map/depth/pallas_call | solution.py:457
  12.3 2.1 %maximum_select_fusion = f32[2,160,640]{2,1,0:T(8,128)} fusion(f32[1,160,640]{2,1,0:T(8,128)} %bitcast.5, f32[1,160,640]{2,1,0:T(8,128)S(1)} %bitcast.40, pred[]{:T(512)S(6)} %eq.9), kind=kLoop, calls=%fused_computation | loop fusion | flops 614400 | bytes 1638401 | tf_op jit(solution)/shard_map/jit(_where)/select_n | solution.py:467
  14.4 5.4 %all-to-all-start = ((f32[8,40,640]{2,1,0:T(8,128)}), f32[8,40,640]{2,1,0:T(8,128)}, u32[]{:S(2)}, u32[]{:S(2)}) async-start(f32[8,40,640]{2,1,0:T(8,128)} %bitcast.43), calls=%async_computation | async-start | bytes 1638400 | tf_op jit(solution)/shard_map/all_to_all | solution.py:472
  19.8 0.1 slice_reduce_fusion
  20.0 9.2 %prepare.1 = (f32[12800,128]{1,0:T(8,128)S(1)}, f32[7680,128]{1,0:T(8,128)S(1)}) custom-call(s32[192]{0:T(256)S(1)} %get-tuple-element.32.box_plane, s32[192]{0:T(256)S(1)} %get-tuple-element.30.box_odd, f32[20,160,160]{2,1,0:T(8,128)S(1)} %copy-done.2, f32[192,128]{1,0:T(8,128)S(1)} %copy-done.7), custom_call_target="tpu_custom_call" | custom-call | bytes 14000000 | tf_op jit(solution)/shard_map/prepare/pallas_call | solution.py:481
  29.2 1.9 %copy-done = f32[7680,128]{1,0:T(8,128)} copy-done((f32[7680,128]{1,0:T(8,128)}, f32[7680,128]{1,0:T(8,128)S(1)}, u32[]{:S(2)}) %copy-start) | copy-done | bytes 3932184
  31.1 2.8 %copy-done.1 = f32[12800,128]{1,0:T(8,128)} copy-done((f32[12800,128]{1,0:T(8,128)}, f32[12800,128]{1,0:T(8,128)S(1)}, u32[]{:S(2)}) %copy-start.1) | copy-done | bytes 6553624
  33.8 0.6 subtract_add_fusion.box_base
  34.4 0.6 fusion.3
  35.0 20.3 %planes_forward.1 = (f32[13440,128]{1,0:T(8,128)S(1)}, f32[8,8,256]{2,1,0:T(8,128)}) custom-call(s32[5120]{0:T(1024)} %get-tuple-element.36.site_row, s32[192]{0:T(256)} %subtract_add_fusion.box_base, f32[8,40,640]{2,1,0:T(8,128)} %all-to-all-done.recv, bf16[160,960]{1,0:T(8,128)(2,1)} %constant.122.clone.first_matrix, ...), custom_call_target="tpu_custom_call" | custom-call | tf_op jit(solution)/shard_map/planes_forward/pallas_call | solution.py:499
  55.3 12.1 %all_to_all.24.shared = f32[8,8,256]{2,1,0:T(8,128)S(1)} all-to-all(f32[8,8,256]{2,1,0:T(8,128)} %get-tuple-element.18), channel_id=1, replica_groups=mesh['band'=16,'ga'=8] {'ga'}, dimensions={0} | all-to-all | bytes 131072 | tf_op jit(solution)/shard_map/all_to_all | solution.py:528
  67.5 20.1 %planes_backward.1 = (f32[8,40,640]{2,1,0:T(8,128)}, f32[13440,128]{1,0:T(8,128)S(1)}) custom-call(s32[5120]{0:T(1024)S(1)} %get-tuple-element.37.site_row, s32[192]{0:T(256)S(1)} %copy-done.8, f32[8,8,256]{2,1,0:T(8,128)S(1)} %all_to_all.24.shared, f32[1,1024]{1,0:T(1,128)S(1)} %bitcast.36, s32[1,192]{1,0:T(1,128)S(1)} %bitcast.38, ...), custom_call_target="tpu_custom_call", output_to_operand_aliasing={{1}: (8, {})} | custom-call | tf_op jit(solution)/shard_map/planes_backward/pallas_call | solution.py:529
  87.6 3.6 %all-to-all-start.2 = ((f32[8,40,640]{2,1,0:T(8,128)}), f32[8,40,640]{2,1,0:T(8,128)S(1)}, u32[]{:S(2)}, u32[]{:S(2)}) async-start(f32[8,40,640]{2,1,0:T(8,128)} %get-tuple-element.20), calls=%async_computation.2 | async-start | bytes 1638400 | tf_op jit(solution)/shard_map/all_to_all | solution.py:557
  91.1 0.1 fusion.9
  91.2 12.2 %all-to-all-done.2 = f32[8,40,640]{2,1,0:T(8,128)S(1)} async-done(((f32[8,40,640]{2,1,0:T(8,128)}), f32[8,40,640]{2,1,0:T(8,128)S(1)}, u32[]{:S(2)}, u32[]{:S(2)}) %all-to-all-start.2) | async-done | bytes 819232 | tf_op jit(solution)/shard_map/all_to_all | solution.py:557
  103.4 1.6 %finish.1 = (f32[320,640]{1,0:T(8,128)}, f32[160,640]{1,0:T(8,128)S(1)}) custom-call(s32[1]{0:T(128)} %bitcast.core, bf16[320,960]{1,0:T(8,128)(2,1)S(1)} %copy-done.4, f32[320,640]{1,0:T(8,128)S(1)} %bitcast.33, f32[320,640]{1,0:T(8,128)S(1)} %bitcast.35, f32[1,640]{1,0:T(1,128)S(1)} %reshape.79.plane_kinetic), custom_call_target="tpu_custom_call" | custom-call | tf_op jit(solution)/shard_map/finish/pallas_call | solution.py:561
  105.1 1.7 %collective-permute-done.1.brought = f32[160,640]{1,0:T(8,128)S(1)} collective-permute-done((f32[160,640]{1,0:T(8,128)S(1)}, f32[160,640]{1,0:T(8,128)S(1)}, u32[]{:S(2)}, u32[]{:S(2)}) %collective-permute-start.1) | collective-permute-done | bytes 409632 | tf_op jit(solution)/shard_map/ppermute | solution.py:575
  106.8 0.8 copy-done.11
  107.6 5.8 %gram.1 = f32[16,32]{1,0:T(8,128)} custom-call(s32[1]{0:T(128)} %bitcast.core, f32[320,640]{1,0:T(8,128)} %get-tuple-element.21.result, f32[160,640]{1,0:T(8,128)} %copy-done.11, f32[8,2,160,640]{3,2,1,0:T(8,128)} %bitcast.39), custom_call_target="tpu_custom_call" | custom-call | tf_op jit(solution)/shard_map/gram/pallas_call | solution.py:576
  113.3 9.5 %all_to_all.25 = f32[16,1,32]{2,1,0:T(1,128)S(1)} all-to-all(f32[16,1,32]{2,1,0:T(1,128)} %bitcast.44), channel_id=1, replica_groups={{0,1,2,3,4,5,6,7,8,9,10,11,12,13,14,15},{16,17,18,19,20,21,22,23,24,25,..., dimensions={0} | all-to-all | bytes 4096 | tf_op jit(solution)/shard_map/all_to_all | solution.py:591
  122.9 0.1 mul.54
  123.0 0.7 copy.25
  (35 shorter events, 0.2 us)
Async XLA Ops:
  7.2 99.6 %all-gather.3.cloned.1.call-start = ((), (), s32[]{:S(2)}) async-start(), calls=%async_computation.4 | async-start | bytes 7372800 | tf_op jit(solution)/shard_map/all_gather | solution.py:471
  7.2 12.6 %copy-start.12 = (s32[192,128]{1,0:T(8,128)S(1)}, s32[192,128]{1,0:T(8,128)}, u32[]{:S(2)}) copy-start(s32[192,128]{1,0:T(8,128)} %param.18) | copy-start | bytes 294916
  7.2 12.7 %copy-start.2 = (f32[20,160,160]{2,1,0:T(8,128)S(1)}, f32[20,160,160]{2,1,0:T(8,128)}, u32[]{:S(2)}) copy-start(f32[20,160,160]{2,1,0:T(8,128)} %potential.1) | copy-start | bytes 6144004
  7.2 12.7 %copy-start.7 = (f32[192,128]{1,0:T(8,128)S(1)}, f32[192,128]{1,0:T(8,128)}, u32[]{:S(2)}) copy-start(f32[192,128]{1,0:T(8,128)} %box_beta.1) | copy-start | bytes 294916
  9.3 2.9 %collective-permute-start = (f32[2,80,640]{2,1,0:T(8,128)}, f32[2,80,640]{2,1,0:T(8,128)}, u32[]{:S(2)}, u32[]{:S(2)}) collective-permute-start(f32[2,80,640]{2,1,0:T(8,128)} %get-tuple-element.34), channel_id=1, source_target_pairs={{0,8},{8,0},{16,24},{24,16},{32,40},{40,32},{48,56},{56,48},{64,72... | collective-permute-start | bytes 1228808 | tf_op jit(solution)/shard_map/ppermute | solution.py:456
  9.3 25.1 %copy-start.13 = (s32[5120]{0:T(1024)S(1)}, s32[5120]{0:T(1024)}, u32[]{:S(2)}) copy-start(s32[5120]{0:T(1024)} %param.16) | copy-start | bytes 61444
  14.4 20.6 %all-to-all-start = ((f32[8,40,640]{2,1,0:T(8,128)}), f32[8,40,640]{2,1,0:T(8,128)}, u32[]{:S(2)}, u32[]{:S(2)}) async-start(f32[8,40,640]{2,1,0:T(8,128)} %bitcast.43), calls=%async_computation | async-start | bytes 1638400 | tf_op jit(solution)/shard_map/all_to_all | solution.py:472
  29.2 1.9 %copy-start = (f32[7680,128]{1,0:T(8,128)}, f32[7680,128]{1,0:T(8,128)S(1)}, u32[]{:S(2)}) copy-start(f32[7680,128]{1,0:T(8,128)S(1)} %get-tuple-element.17.beta_in) | copy-start | bytes 11796484
  31.1 2.8 %copy-start.1 = (f32[12800,128]{1,0:T(8,128)}, f32[12800,128]{1,0:T(8,128)S(1)}, u32[]{:S(2)}) copy-start(f32[12800,128]{1,0:T(8,128)S(1)} %get-tuple-element.16.potential_in) | copy-start | bytes 19660804
  33.8 33.6 %copy-start.5 = (bf16[160,960]{1,0:T(8,128)(2,1)S(1)}, bf16[160,960]{1,0:T(8,128)(2,1)}, u32[]{:S(2)}) copy-start(bf16[160,960]{1,0:T(8,128)(2,1)} %constant.124.clone.first_matrix) | copy-start | bytes 921604
  33.8 33.6 %copy-start.6 = (bf16[160,960]{1,0:T(8,128)(2,1)S(1)}, bf16[160,960]{1,0:T(8,128)(2,1)}, u32[]{:S(2)}) copy-start(bf16[160,960]{1,0:T(8,128)(2,1)} %constant.125.clone.second_matrix) | copy-start | bytes 921604
  33.8 33.6 %copy-start.9 = (f32[1024]{0:T(1024)S(1)}, f32[1024]{0:T(1024)}, u32[]{:S(2)}) copy-start(f32[1024]{0:T(1024)} %param.21) | copy-start | bytes 12292
  33.8 33.6 %copy-start.10 = (s32[192]{0:T(256)S(1)}, s32[192]{0:T(256)}, u32[]{:S(2)}) copy-start(s32[192]{0:T(256)} %param.19) | copy-start | bytes 2308
  34.4 33.0 %copy-start.8 = (s32[192]{0:T(256)S(1)}, s32[192]{0:T(256)}, u32[]{:S(2)}) copy-start(s32[192]{0:T(256)} %subtract_add_fusion.box_base) | copy-start | bytes 2308
  67.5 36.0 %copy-start.3 = (f32[1,2,160,640]{3,2,1,0:T(8,128)S(1)}, f32[1,2,160,640]{3,2,1,0:T(8,128)}, u32[]{:S(2)}) copy-start(f32[1,2,160,640]{3,2,1,0:T(8,128)} %param.14) | copy-start | bytes 2457604
  67.5 36.0 %copy-start.4 = (bf16[320,960]{1,0:T(8,128)(2,1)S(1)}, bf16[320,960]{1,0:T(8,128)(2,1)}, u32[]{:S(2)}) copy-start(bf16[320,960]{1,0:T(8,128)(2,1)} %constant.126.clone.matrix) | copy-start | bytes 1843204
  87.6 15.9 %all-to-all-start.2 = ((f32[8,40,640]{2,1,0:T(8,128)}), f32[8,40,640]{2,1,0:T(8,128)S(1)}, u32[]{:S(2)}, u32[]{:S(2)}) async-start(f32[8,40,640]{2,1,0:T(8,128)} %get-tuple-element.20), calls=%async_computation.2 | async-start | bytes 1638400 | tf_op jit(solution)/shard_map/all_to_all | solution.py:557
  105.1 1.7 %collective-permute-start.1 = (f32[160,640]{1,0:T(8,128)S(1)}, f32[160,640]{1,0:T(8,128)S(1)}, u32[]{:S(2)}, u32[]{:S(2)}) collective-permute-start(f32[160,640]{1,0:T(8,128)S(1)} %get-tuple-element.22), channel_id=1, source_target_pairs={{0,8},{8,0},{16,24},{24,16},{32,40},{40,32},{48,56},{56,48},{64,72... | collective-permute-start | bytes 1228808 | tf_op jit(solution)/shard_map/ppermute | solution.py:575
  106.8 0.8 copy-start.11
Sparse Core Ops, SparseCore 0:
  14.5 86.5 all-gather.2
